TPU v7x, 256 devices: a whole 4x4x8 slice. The times are simulated.
256 devices in a mesh: clips: 16 (over x_hi, y, core), tm: 16 (over z, x_lo).
Axes of the slice: x: 4 (x_hi: 2, x_lo: 2; x = x_hi * 2 + x_lo), y: 4, z: 8, core: 2. Of those that a mesh axis runs over, the one named last changes fastest.
Arguments:
- video: bfloat16 [16, 256, 8, 8, 256], P('clips', 'tm'), may hold values from -6 to 6
- cotangent: bfloat16 [16, 128, 4, 4, 1024], P('clips', 'tm'), may hold values from -0.01171875 to 0.01171875
- gains: float32 [2, 256], replicated, may hold values from 0.5 to 2
- spatial_weights: bfloat16 [2, 3, 3, 256, 256], replicated, may hold values from -0.125 to 0.125
- time_weights: bfloat16 [2, 3, 256, 256], replicated, may hold values from -0.21875 to 0.21875
- reduce_kernel_weights: bfloat16 [3, 256, 256], replicated, may hold values from -0.21875 to 0.21875
Outputs:
- encoded: bfloat16 [16, 128, 4, 4, 1024], P('clips', 'tm')
- grad_spatial: float32 [2, 3, 3, 256, 256], replicated
- grad_time: float32 [2, 3, 256, 256], replicated
- grad_down: float32 [3, 256, 256], replicated
- grad_gains: float32 [2, 256], replicated
All inputs are finite; a program needn't handle non-finite values.
Results may differ from a plain program's by a relative error of at most 0.017.
Values may be sent and summed in bfloat16 or wider, within the bound.
No kernel may reach another device: no remote copies, remote signals or barrier semaphores. Data moves between devices by JAX's collectives and lax.ppermute only.
A program may use at most 128 MiB of HBM per device.

v0:
```python
import jax
import jax.numpy as jnp
from jax import lax
from jax.sharding import PartitionSpec as P

EPSILON = 1e-06


def passed_along(value, axis, steps):
    count = lax.axis_size(axis)
    first, last = (max(0, -steps), min(count, count - steps))
    return lax.ppermute(value, axis, [(source, source + steps) for source in range(first, last)])


def normed(stream, gain):
    scale_inv = lax.rsqrt(jnp.mean(stream * stream, axis=-1, keepdims=True) + EPSILON)
    return stream * scale_inv * gain


def pad_space(values):
    return jnp.pad(values, ((0, 0), (0, 0), (1, 1), (1, 1), (0, 0)))


def spatial(normed_in, weight_tensors):
    side_len = normed_in.shape[2]
    padded = pad_space(normed_in)
    summed = jnp.zeros(normed_in.shape[:-1] + (weight_tensors.shape[-1],), jnp.float32)
    for row_shift in range(3):
        for col_shift in range(3):
            window = padded[
                :, :, row_shift : row_shift + side_len, col_shift : col_shift + side_len
            ]
            summed = summed + jnp.dot(
                window, weight_tensors[row_shift, col_shift], preferred_element_type=jnp.float32
            )
    return summed


def outer_sum(left, right):
    return lax.dot_general(
        left.reshape(-1, left.shape[-1]),
        right.reshape(-1, right.shape[-1]),
        (((0,), (0,)), ((), ())),
        preferred_element_type=jnp.float32,
    )


def spatial_grad(normed_in, grad_pre, weight_tensors):
    side_len = normed_in.shape[2]
    padded_in = pad_space(normed_in)
    padded_grad = pad_space(grad_pre)
    grad_norm = jnp.zeros(normed_in.shape, jnp.float32)
    rows_out = []
    for row_shift in range(3):
        cols_out = []
        for col_shift in range(3):
            window = padded_in[
                :, :, row_shift : row_shift + side_len, col_shift : col_shift + side_len
            ]
            cols_out.append(outer_sum(window, grad_pre))
            back = padded_grad[
                :,
                :,
                2 - row_shift : 2 - row_shift + side_len,
                2 - col_shift : 2 - col_shift + side_len,
            ]
            grad_norm = grad_norm + jnp.dot(
                back, weight_tensors[row_shift, col_shift].T, preferred_element_type=jnp.float32
            )
        rows_out.append(jnp.stack(cols_out))
    return (jnp.stack(rows_out), grad_norm)


def silu_slope(conv_out):
    logistic = jax.nn.sigmoid(conv_out)
    return logistic * (1.0 + conv_out * (1.0 - logistic))


def norm_back(stream, gain, grad_norm):
    _, pullback = jax.vjp(normed, stream, gain)
    return pullback(grad_norm)


def section_in(stream, gain, weight_tensors):
    normed_in = normed(stream, gain).astype(jnp.bfloat16)
    conv_out = spatial(normed_in, weight_tensors)
    activated = jax.nn.silu(conv_out).astype(jnp.bfloat16)
    return (normed_in, conv_out, activated)


def temporal(with_edge, weight_tensors):
    frame_count = with_edge.shape[1] - 2
    summed = jnp.zeros(
        (with_edge.shape[0], frame_count) + with_edge.shape[2:-1] + (weight_tensors.shape[-1],),
        jnp.float32,
    )
    for kernel_tap in range(3):
        summed = summed + jnp.dot(
            with_edge[:, 2 - kernel_tap : 2 - kernel_tap + frame_count],
            weight_tensors[kernel_tap],
            preferred_element_type=jnp.float32,
        )
    return summed


def regroup(values):
    clips, halves, side_len, _, channels = values.shape
    split = values.reshape(clips, halves, side_len // 2, 2, side_len // 2, 2, channels)
    return split.transpose(0, 1, 2, 4, 3, 5, 6).reshape(
        clips, halves, side_len // 2, side_len // 2, 4 * channels
    )


def ungroup(values):
    clips, halves, half_side, _, wide_channels = values.shape
    channels = wide_channels // 4
    split = values.reshape(clips, halves, half_side, half_side, 2, 2, channels)
    return split.transpose(0, 1, 2, 4, 3, 5, 6).reshape(
        clips, halves, 2 * half_side, 2 * half_side, channels
    )


def block_back(stored_block, upstream, gain, spatial_w, time_w):
    stream_in, normed_in, conv_out, with_edge = stored_block
    grad_bf = upstream.astype(jnp.bfloat16)
    later_edge = passed_along(grad_bf[:, :2], "tm", -1)
    frame_count = grad_bf.shape[1]
    grad_tm = jnp.stack(
        [
            outer_sum(with_edge[:, 2 - kernel_tap : 2 - kernel_tap + frame_count], grad_bf)
            for kernel_tap in range(3)
        ]
    )
    padded_later = jnp.concatenate([grad_bf, later_edge], axis=1)
    grad_act = jnp.zeros(grad_bf.shape, jnp.float32)
    for kernel_tap in range(3):
        grad_act = grad_act + jnp.dot(
            padded_later[:, kernel_tap : kernel_tap + frame_count],
            time_w[kernel_tap].T,
            preferred_element_type=jnp.float32,
        )
    grad_pre = (grad_act * silu_slope(conv_out)).astype(jnp.bfloat16)
    grad_sp, grad_norm = spatial_grad(normed_in, grad_pre, spatial_w)
    grad_stream, grad_gain = norm_back(stream_in, gain, grad_norm)
    return (upstream + grad_stream, grad_sp, grad_tm, grad_gain)


def on_device(video, cotangent, gains, spatial_weights, time_weights, reduce_kernel_weights):
    block_count = spatial_weights.shape[0]
    cot_frames = ungroup(cotangent)
    cot_after = passed_along(cot_frames[:, :1], "tm", -1)
    stream = video.astype(jnp.float32)
    stored = []
    for which_block in range(block_count):
        normed_in, conv_out, activated = section_in(
            stream, gains[which_block], spatial_weights[which_block]
        )
        edge_act = passed_along(activated[:, -2:], "tm", 1)
        with_edge = jnp.concatenate([edge_act, activated], axis=1)
        stored.append((stream, normed_in, conv_out, with_edge))
        stream = stream + temporal(with_edge, time_weights[which_block])
    lowered_program = stream.astype(jnp.bfloat16)
    preceding_odd_frame = passed_along(lowered_program[:, -1:], "tm", 1)
    clips, frame_count, side_len, _, channels = lowered_program.shape
    frame_pairs = lowered_program.reshape(clips, frame_count // 2, 2, side_len, side_len, channels)
    even_frames = frame_pairs[:, :, 0]
    odd_frames = frame_pairs[:, :, 1]
    prev_frames = jnp.concatenate([preceding_odd_frame, odd_frames[:, :-1]], axis=1)
    encoded_result = jnp.dot(
        odd_frames, reduce_kernel_weights[0], preferred_element_type=jnp.float32
    )
    encoded_result = encoded_result + jnp.dot(
        even_frames, reduce_kernel_weights[1], preferred_element_type=jnp.float32
    )
    encoded_result = encoded_result + jnp.dot(
        prev_frames, reduce_kernel_weights[2], preferred_element_type=jnp.float32
    )
    encoded = regroup(encoded_result.astype(jnp.bfloat16))
    grad_dn = jnp.stack(
        [
            outer_sum(odd_frames, cot_frames),
            outer_sum(even_frames, cot_frames),
            outer_sum(prev_frames, cot_frames),
        ]
    )
    cot_next = jnp.concatenate([cot_frames[:, 1:], cot_after], axis=1)
    grad_odd = jnp.dot(cot_frames, reduce_kernel_weights[0].T, preferred_element_type=jnp.float32)
    grad_odd = grad_odd + jnp.dot(
        cot_next, reduce_kernel_weights[2].T, preferred_element_type=jnp.float32
    )
    grad_even = jnp.dot(cot_frames, reduce_kernel_weights[1].T, preferred_element_type=jnp.float32)
    upstream = jnp.stack([grad_even, grad_odd], axis=2).reshape(
        clips, frame_count, side_len, side_len, channels
    )
    list_sp, list_tm, list_gn = ([], [], [])
    for which_block in reversed(range(block_count)):
        upstream, grad_sp, grad_tm, grad_gain = block_back(
            stored[which_block],
            upstream,
            gains[which_block],
            spatial_weights[which_block],
            time_weights[which_block],
        )
        list_sp.append(grad_sp)
        list_tm.append(grad_tm)
        list_gn.append(grad_gain)
    local_grads = (
        jnp.stack(list_sp[::-1]),
        jnp.stack(list_tm[::-1]),
        grad_dn,
        jnp.stack(list_gn[::-1]),
    )
    summed_grads = lax.psum(
        (local_grads[0], local_grads[1], local_grads[2], local_grads[3]), ("clips", "tm")
    )
    return (encoded, summed_grads[0], summed_grads[1], summed_grads[2], summed_grads[3])


def solution(mesh):
    placed = (
        P("clips", "tm", None, None, None),
        P("clips", "tm", None, None, None),
        P(),
        P(),
        P(),
        P(),
    )
    return jax.shard_map(
        on_device,
        mesh=mesh,
        in_specs=placed,
        out_specs=(P("clips", "tm", None, None, None), P(), P(), P(), P()),
        check_vma=False,
    )
```

profile of v0, /device:TPU:1, one launch (start us, length us, event | category | flops | bytes accessed | tf_op | source)
XLA Modules:
  0.0 371.3 jit_solution(4967336291081242807)
XLA Ops:
  7.2 1.1 reshape.589
  8.7 0.6 slice.425
  9.3 1.3 collective-permute-start.3
  10.9 1.8 slice_bitcast_fusion
  15.5 1.4 multiply_convert_fusion.2
  16.9 0.6 slice.405
  17.5 5.2 %collective-permute-start = (bf16[1,2,8,8,256]{4,3,2,1,0:T(8,128)(2,1)}, bf16[1,2,8,8,256]{4,3,2,1,0:T(8,128)(2,1)}, u32[]{:S(2)}, u32[]{:S(2)}) collective-permute-start(bf16[1,2,8,8,256]{4,3,2,1,0:T(8,128)(2,1)} %slice.405), channel_id=1, source_target_pairs={{0,1},{1,2},{2,3},{3,4},{4,5},{5,6},{6,7},{7,8},{8,9},{9,10},{10,1... | collective-permute-start | bytes 196616 | tf_op jit(solution)/shard_map/ppermute | solution.py:12
  22.8 2.3 fusion.146
  25.1 1.1 fusion.158
  26.2 1.2 convolution_bitcast_fusion
  27.4 1.1 reshape_reshape.2
  28.4 1.0 slice.424
  29.4 1.4 fusion.12
  31.2 1.4 collective-permute-start.4
  33.0 1.1 convolution_add_fusion.31
  34.1 1.3 multiply_reduce_fusion
  38.2 0.5 multiply_convert_fusion
  39.3 4.5 %collective-permute-start.1 = (bf16[1,2,8,8,256]{4,3,2,1,0:T(8,128)(2,1)S(1)}, bf16[1,2,8,8,256]{4,3,2,1,0:T(8,128)(2,1)S(1)}, u32[]{:S(2)}, u32[]{:S(2)}) collective-permute-start(bf16[1,2,8,8,256]{4,3,2,1,0:T(8,128)(2,1)S(1)} %slice.417), channel_id=1, source_target_pairs={{0,1},{1,2},{2,3},{3,4},{4,5},{5,6},{6,7},{7,8},{8,9},{9,10},{10,1... | collective-permute-start | bytes 196616 | tf_op jit(solution)/shard_map/ppermute | solution.py:12
  44.2 0.6 fusion.8
  44.7 0.4 convolution_bitcast_fusion.10
  45.4 0.4 convolution_bitcast_fusion.12
  45.8 0.3 convolution_bitcast_fusion.13
  46.5 0.3 convolution_bitcast_fusion.15
  46.9 0.3 convolution_bitcast_fusion.16
  47.6 0.3 convolution_bitcast_fusion.18
  47.9 0.3 fusion.47
  48.6 0.3 convolution_add_fusion.16
  49.0 0.3 convolution_add_fusion.15
  49.7 0.3 convolution_add_fusion.13
  50.0 0.3 convolution_add_fusion.12
  50.7 0.6 fusion.18
  51.7 0.3 convolution_bitcast_fusion.9
  52.4 1.3 collective-permute-start.5
  54.1 1.1 convolution_bitcast_fusion.8
  55.2 1.2 convolution_bitcast_fusion.7
  57.2 5.1 %collective-permute-start.2 = (bf16[1,1,8,8,256]{4,3,2,1,0:T(8,128)(2,1)S(1)}, bf16[1,1,8,8,256]{4,3,2,1,0:T(8,128)(2,1)S(1)}, u32[]{:S(2)}, u32[]{:S(2)}) collective-permute-start(bf16[1,1,8,8,256]{4,3,2,1,0:T(8,128)(2,1)S(1)} %slice.422), channel_id=1, source_target_pairs={{0,1},{1,2},{2,3},{3,4},{4,5},{5,6},{6,7},{7,8},{8,9},{9,10},{10,1... | collective-permute-start | bytes 98312 | tf_op jit(solution)/shard_map/ppermute | solution.py:12
  62.4 0.4 convolution_bitcast_fusion.5
  62.8 0.4 convolution_bitcast_fusion.4
  63.2 1.3 pad_maximum_fusion.1
  65.5 0.9 copy-done.16
  66.4 0.6 fusion.9
  66.9 0.4 convolution_bitcast_fusion.19
  67.7 0.4 convolution_bitcast_fusion.21
  68.0 0.3 convolution_bitcast_fusion.22
  68.7 0.3 convolution_bitcast_fusion.24
  69.1 0.3 convolution_bitcast_fusion.25
  69.8 0.3 convolution_bitcast_fusion.27
  70.8 2.6 pad_maximum_fusion
  73.4 0.9 pad_maximum_fusion.3
  74.3 1.0 copy-done.10
  75.8 1.2 fusion.13
  77.3 0.9 reshape.588
  78.9 0.3 convolution_add_fusion.6
  79.3 0.3 convolution_add_fusion.5
  80.0 0.3 convolution_add_fusion.3
  80.3 0.3 convolution_add_fusion.2
  81.0 0.7 copy-done.3
  81.7 0.4 fusion.11
  82.2 84.4 %psum.31 = f32[2,256]{1,0:T(2,128)} all-reduce(f32[2,256]{1,0:T(2,128)S(1)} %pad_maximum_fusion.9), channel_id=1, replica_groups=mesh['clips'=16,'tm'=16] {'clips','tm'}, use_global_device_ids=true, to_apply=%region_8.9 | all-reduce | flops 512 | bytes 4096 | tf_op jit(solution)/shard_map/psum | solution.py:213
  166.5 190.3 %all-reduce.7.cloned.1.call-done = (f32[2,3,3,256,256]{4,3,2,1,0:T(8,128)}, f32[2,3,256,256]{3,2,1,0:T(8,128)}, f32[3,256,256]{2,1,0:T(8,128)}) async-done(((f32[2,3,3,256,256]{4,3,2,1,0:T(8,128)}, f32[2,3,256,256]{3,2,1,0:T(8,128)}, f32[3,256,256]{2,1,0:T(8,128)}), (f32[2,3,3,256,256]{4,3,2,1,0:T(8,128)}, f32[2,3,256,256]{3,2,1,0:T(8,128)}, f32[3,256,256]{2,1,0:T(8,128)})) %all-reduce.7.cloned.1.call-update) | async-done | bytes 7077904 | tf_op jit(solution)/shard_map/psum | solution.py:213
  356.8 5.0 %copy.224 = f32[2,3,3,256,256]{4,3,2,1,0:T(8,128)} copy(f32[2,3,3,256,256]{4,3,2,1,0:T(8,128)} %get-tuple-element.29) | data formatting | bytes 9437184
  361.9 1.1 copy.225
  363.0 0.5 copy-done.12
  363.6 0.9 copy.226
  (114 shorter events, 16.4 us)
Async XLA Ops:
  7.2 3.4 copy-start.15
  7.2 3.4 copy-start.2
  7.2 349.6 %all-reduce.7.cloned.1.call-start = ((), (), s32[]{:S(2)}) async-start(), calls=%async_computation | async-start | bytes 14155776 | tf_op jit(solution)/shard_map/psum | solution.py:213
  8.5 14.2 %copy-start.4 = (bf16[1,8,4,4,2,2,256]{6,5,3,4,2,1,0:T(2,128)(2,1)}, bf16[1,8,4,4,2,2,256]{6,5,3,4,2,1,0:T(2,128)(2,1)S(1)}, u32[]{:S(2)}) copy-start(bf16[1,8,4,4,2,2,256]{6,5,3,4,2,1,0:T(2,128)(2,1)S(1)} %copy.220) | copy-start | bytes 786436
  8.7 4.1 %copy-start.11 = (bf16[1,8,8,8,256]{4,3,2,1,0:T(8,128)(2,1)}, bf16[1,8,8,8,256]{4,3,2,1,0:T(8,128)(2,1)S(1)}, u32[]{:S(2)}) copy-start(bf16[1,8,8,8,256]{4,3,2,1,0:T(8,128)(2,1)S(1)} %reshape.591) | copy-start | bytes 786436
  9.3 20.1 %collective-permute-start.3 = (bf16[1,1,8,8,256]{4,3,2,1,0:T(8,128)(2,1)}, bf16[1,1,8,8,256]{4,3,2,1,0:T(8,128)(2,1)}, u32[]{:S(2)}, u32[]{:S(2)}) collective-permute-start(bf16[1,1,8,8,256]{4,3,2,1,0:T(8,128)(2,1)} %slice.425), channel_id=1, source_target_pairs={{1,0},{2,1},{3,2},{4,3},{5,4},{6,5},{7,6},{8,7},{9,8},{10,9},{11,1... | collective-permute-start | bytes 98312 | tf_op jit(solution)/shard_map/ppermute | solution.py:12
  10.9 1.9 copy-start.13
  12.7 2.8 copy-start
  17.5 15.5 %collective-permute-start = (bf16[1,2,8,8,256]{4,3,2,1,0:T(8,128)(2,1)}, bf16[1,2,8,8,256]{4,3,2,1,0:T(8,128)(2,1)}, u32[]{:S(2)}, u32[]{:S(2)}) collective-permute-start(bf16[1,2,8,8,256]{4,3,2,1,0:T(8,128)(2,1)} %slice.405), channel_id=1, source_target_pairs={{0,1},{1,2},{2,3},{3,4},{4,5},{5,6},{6,7},{7,8},{8,9},{9,10},{10,1... | collective-permute-start | bytes 196616 | tf_op jit(solution)/shard_map/ppermute | solution.py:12
  22.8 2.3 copy-start.6
  22.8 2.3 copy-start.9
  31.1 1.6 copy-start.7
  31.2 1.8 copy-start.5
  31.2 12.6 %collective-permute-start.4 = (bf16[1,2,8,8,256]{4,3,2,1,0:T(8,128)(2,1)S(1)}, bf16[1,2,8,8,256]{4,3,2,1,0:T(8,128)(2,1)S(1)}, u32[]{:S(2)}, u32[]{:S(2)}) collective-permute-start(bf16[1,2,8,8,256]{4,3,2,1,0:T(8,128)(2,1)S(1)} %slice.426), channel_id=1, source_target_pairs={{1,0},{2,1},{3,2},{4,3},{5,4},{6,5},{7,6},{8,7},{9,8},{10,9},{11,1... | collective-permute-start | bytes 196616 | tf_op jit(solution)/shard_map/ppermute | solution.py:12
  39.3 17.2 %collective-permute-start.1 = (bf16[1,2,8,8,256]{4,3,2,1,0:T(8,128)(2,1)S(1)}, bf16[1,2,8,8,256]{4,3,2,1,0:T(8,128)(2,1)S(1)}, u32[]{:S(2)}, u32[]{:S(2)}) collective-permute-start(bf16[1,2,8,8,256]{4,3,2,1,0:T(8,128)(2,1)S(1)} %slice.417), channel_id=1, source_target_pairs={{0,1},{1,2},{2,3},{3,4},{4,5},{5,6},{6,7},{7,8},{8,9},{9,10},{10,1... | collective-permute-start | bytes 196616 | tf_op jit(solution)/shard_map/ppermute | solution.py:12
  52.4 12.7 %collective-permute-start.5 = (bf16[1,2,8,8,256]{4,3,2,1,0:T(8,128)(2,1)S(1)}, bf16[1,2,8,8,256]{4,3,2,1,0:T(8,128)(2,1)S(1)}, u32[]{:S(2)}, u32[]{:S(2)}) collective-permute-start(bf16[1,2,8,8,256]{4,3,2,1,0:T(8,128)(2,1)S(1)} %slice.429), channel_id=1, source_target_pairs={{1,0},{2,1},{3,2},{4,3},{5,4},{6,5},{7,6},{8,7},{9,8},{10,9},{11,1... | collective-permute-start | bytes 196616 | tf_op jit(solution)/shard_map/ppermute | solution.py:12
  57.2 13.0 %collective-permute-start.2 = (bf16[1,1,8,8,256]{4,3,2,1,0:T(8,128)(2,1)S(1)}, bf16[1,1,8,8,256]{4,3,2,1,0:T(8,128)(2,1)S(1)}, u32[]{:S(2)}, u32[]{:S(2)}) collective-permute-start(bf16[1,1,8,8,256]{4,3,2,1,0:T(8,128)(2,1)S(1)} %slice.422), channel_id=1, source_target_pairs={{0,1},{1,2},{2,3},{3,4},{4,5},{5,6},{6,7},{7,8},{8,9},{9,10},{10,1... | collective-permute-start | bytes 98312 | tf_op jit(solution)/shard_map/ppermute | solution.py:12
  65.2 1.2 copy-start.16
  74.3 1.0 copy-start.10
  75.8 2.4 copy-start.1
  80.7 1.0 copy-start.3
  80.7 1.0 copy-start.14
  356.8 5.0 %copy-start.8 = (f32[2,3,256,256]{3,2,1,0:T(8,128)S(1)}, f32[2,3,256,256]{3,2,1,0:T(8,128)}, u32[]{:S(2)}) copy-start(f32[2,3,256,256]{3,2,1,0:T(8,128)} %get-tuple-element.30) | copy-start | bytes 4718596
  361.9 1.7 copy-start.12
Sparse Core Ops, SparseCore 0:
  74.5 282.3 all-reduce.6
where the time goes:
time: 373 us; the launch traced here: 371 us
  waiting for transfers between devices  190 us (51%)
  blocking collectives  84.4 us (23%)
  matrix products  37.6 us (10%)
  starting transfers between devices  18.8 us (5%)
  local copies, waits for them, and re-layouts  18.2 us (5%)
  between operations  15.1 us (4%)
  other arithmetic  6.9 us (2%)
    psum x1, waiting for transfers between devices, on_device(): lax.psum((local_grads[0], local_grads[1], local_grads[2], local_grads[3])...  190 us
    psum x1, blocking collectives, on_device(): lax.psum((local_grads[0], local_grads[1], local_grads[2], local_grads[3])...  84.4 us
    ppermute x6, starting transfers between devices, passed_along(): lax.ppermute(value, axis, [(source, source + steps) for source in range(f...  18.8 us
    dot_general x27, matrix products, outer_sum(): lax.dot_general(left.reshape(-1, left.shape[-1]), right.reshape(-1, right...  10.9 us
    unnamed x37, local copies, waits for them, and re-layouts  10.2 us
  transfers between devices with their start and end apart: 7, of which 1 were waited for; matrix products, arithmetic and copies ran while one was open for 12% of the time, Pallas kernels for 0%

commit v1 on v0

v1 whole, which is shorter than its diff:
```python
import jax
import jax.numpy as jnp
from jax import lax
from jax.experimental import pallas as pl
from jax.experimental.pallas import tpu as pltpu
from jax.sharding import Mesh, PartitionSpec as P

EPSILON = 1e-06
F32 = jnp.float32
BF16 = jnp.bfloat16
C = 256
PIX = 64
FR = 16
MATS = 27
ROWS = MATS * C
CHUNK = 448
FLAT = 16 * CHUNK
EVERY = ("xh", "y", "core", "z", "xl")
PLANE = ("xh", "xl", "y")


def dot(left, right):
    return jnp.dot(left, right, preferred_element_type=F32)


def dot_nt(left, right):
    return lax.dot_general(left, right, (((1,), (1,)), ((), ())), preferred_element_type=F32)


def dot_tn(left, right):
    return lax.dot_general(left, right, (((0,), (0,)), ((), ())), preferred_element_type=F32)


def frames(first, count):
    return pl.ds(first * PIX, count * PIX)


def one_frame(index):
    return pl.ds(pl.multiple_of(index * PIX, PIX), PIX)


def write_windows(value, im_ref, rows, sign):
    grid = value.reshape(8, 8, C)
    column = lax.broadcasted_iota(jnp.int32, (8, 8, C), 1)
    blank = jnp.zeros((1, 8, C), F32)
    for j in range(3):
        dx = sign * (j - 1)
        if dx == 0:
            moved = grid
        elif dx == 1:
            moved = jnp.where(column == 7, 0.0, pltpu.roll(grid, 7, 1))
        else:
            moved = jnp.where(column == 0, 0.0, pltpu.roll(grid, 1, 1))
        for i in range(3):
            dy = sign * (i - 1)
            if dy == 0:
                placed = moved
            elif dy == 1:
                placed = jnp.concatenate([moved[1:], blank], axis=0)
            else:
                placed = jnp.concatenate([blank, moved[:-1]], axis=0)
            tap = 3 * i + j
            im_ref[rows, tap * C : (tap + 1) * C] = placed.reshape(PIX, C).astype(BF16)


def place_matrix(groups):
    size = groups * 8
    dest = lax.broadcasted_iota(jnp.int32, (size, size), 0)
    src = lax.broadcasted_iota(jnp.int32, (size, size), 1)
    want = (dest & 1) * (groups * 4) + (dest >> 3) * 4 + ((dest >> 1) & 3)
    return jnp.where(src == want, 1.0, 0.0).astype(BF16)


def ungroup(cot_ref, groups, one_hot):
    halves = []
    for i in range(2):
        both = jnp.concatenate(
            [cot_ref[:, (2 * i + j) * C : (2 * i + j + 1) * C] for j in range(2)], axis=0
        )
        halves.append(dot(one_hot, both).reshape(groups, 8, C))
    return jnp.concatenate(halves, axis=1).reshape(groups * 16, C).astype(BF16)


def model_kernel(
    video_ref,
    before_ref,
    after_ref,
    cot_ref,
    cot_after_ref,
    gains_ref,
    sw_ref,
    tw_ref,
    rw_ref,
    enc_ref,
    grad_ref,
    s1,
    s2,
    im,
    n_refs,
    a1,
    a2,
    slope1,
    slope2,
    low,
    cotf,
    up,
    g2,
    g1,
    ga,
    gn,
    wcat,
):
    s1[frames(0, 6), :] = before_ref[...].astype(F32)
    s1[frames(6, 16), :] = video_ref[...].astype(F32)
    s1[frames(22, 2), :] = after_ref[...].astype(F32)

    def put(matrix, value):
        rows = pl.ds(matrix * C, C)
        for half in range(2):
            grad_ref[half, rows, :] = value[:, half * 128 : (half + 1) * 128].astype(BF16)

    def norm_windows(src, count, own, gain, n_ref):
        def body(index, _):
            rows = one_frame(index)
            value = src[rows, :]
            inv = lax.rsqrt(jnp.mean(value * value, axis=-1, keepdims=True) + EPSILON)
            value = value * inv * gain
            write_windows(value, im, rows, 1)

            @pl.when((index >= own) & (index < own + FR))
            def _():
                n_ref[one_frame(index - own), :] = value.astype(BF16)

            return 0

        lax.fori_loop(0, count, body, 0)

    def activate(block, pieces, act, slope):
        weights = sw_ref[block].reshape(9 * C, C)
        for first, size in pieces:
            rows = pl.ds(first, size)
            conv = dot(im[rows, :], weights)
            logistic = jax.nn.sigmoid(conv)
            act[rows, :] = (conv * logistic).astype(BF16)
            slope[rows, :] = logistic * (1.0 + conv * (1.0 - logistic))

    def temporal(act, first, count, block):
        with_edge = jnp.concatenate([act[frames(first - k, count), :] for k in range(3)], axis=1)
        return dot(with_edge, tw_ref[block].reshape(3 * C, C))

    norm_windows(s1, 24, 6, gains_ref[0:1, :], n_refs.at[0])
    activate(0, [(0, 768), (768, 768)], a1, slope1)
    for first, count in ((0, 11), (11, 10)):
        s2[frames(first, count), :] = s1[frames(first + 3, count), :] + temporal(
            a1, first + 3, count, 0
        )
    norm_windows(s2, 21, 3, gains_ref[1:2, :], n_refs.at[1])
    activate(1, [(0, 672), (672, 672)], a2, slope2)
    low[frames(0, 17), :] = (s2[frames(2, 17), :] + temporal(a2, 2, 17, 1)).astype(BF16)
    low[frames(17, 1), :] = jnp.zeros((PIX, C), BF16)

    pairs = low[...].reshape(9, 2 * PIX, C)
    taps = jnp.concatenate(
        [
            pairs[1:9, :PIX].reshape(8 * PIX, C),
            pairs[0:8, PIX:].reshape(8 * PIX, C),
            pairs[0:8, :PIX].reshape(8 * PIX, C),
        ],
        axis=1,
    )
    one_hot = place_matrix(32)
    down = dot(taps, rw_ref[...].reshape(3 * C, C)).astype(BF16).astype(F32)
    down = down.reshape(32, 16, C)
    for i in range(2):
        both = dot_tn(one_hot, down[:, i * 8 : (i + 1) * 8].reshape(256, C).astype(BF16))
        for j in range(2):
            tap = 2 * i + j
            enc_ref[:, tap * C : (tap + 1) * C] = both[j * 128 : (j + 1) * 128].astype(BF16)
    cotf[frames(0, 8), :] = ungroup(cot_ref, 32, one_hot)
    cotf[frames(8, 3), :] = ungroup(cot_after_ref, 12, place_matrix(12))
    grad_down = dot_tn(taps, cotf[frames(0, 8), :])
    for k in range(3):
        put(24 + k, grad_down[k * C : (k + 1) * C])
    even = dot_nt(cotf[frames(0, 10), :], rw_ref[1])
    odd = dot_nt(cotf[frames(0, 10), :], rw_ref[0]) + dot_nt(cotf[frames(1, 10), :], rw_ref[2])
    merged = jnp.concatenate(
        [even.reshape(10, PIX, C), odd.reshape(10, PIX, C)], axis=1
    ).reshape(20 * PIX, C)
    up[...] = merged[: 18 * PIX]
    g2[...] = merged.astype(BF16)

    def block_back(block, grad, act, own, slope, count, pieces):
        with_edge = jnp.concatenate([act[frames(own - k, FR), :] for k in range(3)], axis=1)
        grad_time = dot_tn(with_edge, grad[frames(0, FR), :])
        for k in range(3):
            put(18 + 3 * block + k, grad_time[k * C : (k + 1) * C])
        for k in range(3):
            wcat[:, k * C : (k + 1) * C] = tw_ref[block, k]
        for first, size in pieces:
            later = jnp.concatenate(
                [grad[pl.ds(first + k * PIX, size), :] for k in range(3)], axis=1
            )
            ga[pl.ds(first, size), :] = dot_nt(later, wcat[:, : 3 * C])

        def body(index, _):
            rows = one_frame(index)
            write_windows(ga[rows, :] * slope[one_frame(index + own), :], im, rows, -1)
            return 0

        lax.fori_loop(0, count, body, 0)
        for tap in range(9):
            wcat[:, tap * C : (tap + 1) * C] = sw_ref[block, tap]
        for first, size in pieces:
            gn[pl.ds(first, size), :] = dot_nt(im[pl.ds(first, size), :], wcat[...])
        for i in range(3):
            grad_sp = dot_tn(n_refs[block], im[frames(0, FR), 3 * i * C : 3 * (i + 1) * C])
            for j in range(3):
                put(9 * block + 3 * i + j, grad_sp[:, j * C : (j + 1) * C])

    def gain_part(index, src, own):
        value = src[one_frame(index + own), :]
        inv = lax.rsqrt(jnp.mean(value * value, axis=-1, keepdims=True) + EPSILON)
        unit = value * inv
        grad = gn[one_frame(index), :]
        return grad, unit, inv

    block_back(1, g2, a2, 3, slope2, 18, [(0, 576), (576, 576)])
    gain = gains_ref[1:2, :]

    def norm_back(index, total):
        grad, unit, inv = gain_part(index, s2, 3)
        scaled = grad * gain
        back = inv * (scaled - unit * jnp.mean(unit * scaled, axis=-1, keepdims=True))
        rows = one_frame(index)
        g1[rows, :] = (up[rows, :] + back).astype(BF16)
        return total + jnp.sum((grad * unit).reshape(8, 8, C), axis=0)

    none = jnp.zeros((8, C), F32)
    total2 = lax.fori_loop(0, FR, norm_back, none)
    lax.fori_loop(FR, FR + 2, norm_back, none)

    block_back(0, g1, a1, 6, slope1, 16, [(0, 512), (512, 512)])

    def gain_only(index, total):
        grad, unit, _ = gain_part(index, s1, 6)
        return total + jnp.sum((grad * unit).reshape(8, 8, C), axis=0)

    total1 = lax.fori_loop(0, FR, gain_only, none)
    rest = jnp.concatenate(
        [
            jnp.sum(total1, axis=0, keepdims=True),
            jnp.sum(total2, axis=0, keepdims=True),
            jnp.zeros((14, C), F32),
        ],
        axis=0,
    )
    for half in range(2):
        grad_ref[half, ROWS : ROWS + 16, :] = rest[:, half * 128 : (half + 1) * 128].astype(BF16)
        grad_ref[half, ROWS + 16 :, :] = jnp.zeros((FLAT - ROWS - 16, 128), BF16)


def run_model(video, before, after, cot, cot_after, gains, sw, tw, rw):
    def vm(rows, dtype, cols=C):
        return pltpu.VMEM((rows * PIX, cols), dtype)

    whole = pl.BlockSpec(memory_space=pltpu.VMEM)
    return pl.pallas_call(
        model_kernel,
        out_shape=(
            jax.ShapeDtypeStruct((128, 4 * C), BF16),
            jax.ShapeDtypeStruct((2, FLAT, 128), BF16),
        ),
        in_specs=[whole] * 9,
        out_specs=(whole, whole),
        scratch_shapes=[
            vm(24, F32),
            vm(21, F32),
            vm(24, BF16, 9 * C),
            pltpu.VMEM((2, FR * PIX, C), BF16),
            vm(24, BF16),
            vm(21, BF16),
            vm(24, F32),
            vm(21, F32),
            vm(18, BF16),
            vm(11, BF16),
            vm(18, F32),
            vm(20, BF16),
            vm(18, BF16),
            vm(18, F32),
            vm(18, F32),
            pltpu.VMEM((C, 9 * C), BF16),
        ],
        compiler_params=pltpu.CompilerParams(vmem_limit_bytes=56 * 1024 * 1024),
        cost_estimate=pl.CostEstimate(
            flops=12_000_000_000, bytes_accessed=10_000_000, transcendentals=1_000_000
        ),
    )(video, before, after, cot, cot_after, gains, sw, tw, rw)


def passed_along(value, axes, steps):
    count = lax.axis_size(axes)
    first, last = (max(0, -steps), min(count, count - steps))
    return lax.ppermute(value, axes, [(source, source + steps) for source in range(first, last)])


def exchange(value, axes):
    return lax.all_to_all(value, axes, split_axis=0, concat_axis=0, tiled=True)


def to_all(value, axes, count):
    rows, cols = value.shape
    copies = jnp.broadcast_to(value[None], (count, rows, cols)).reshape(count * rows, cols)
    return exchange(copies, axes)


def on_device(video, cotangent, gains, spatial_weights, time_weights, reduce_kernel_weights):
    tm = ("z", "xl")
    video = video.reshape(FR * PIX, C)
    cot = cotangent.reshape(FR * 8, 4 * C)
    before = passed_along(video[-6 * PIX :], tm, 1)
    after = passed_along(video[: 2 * PIX], tm, -1)
    cot_after = passed_along(cot[: 3 * 16], tm, -1)
    encoded, grads = run_model(
        video,
        before,
        after,
        cot,
        cot_after,
        gains,
        spatial_weights.reshape(2, 9, C, C),
        time_weights,
        reduce_kernel_weights,
    )
    core = lax.axis_index("core")
    swap = [(0, 1), (1, 0)]
    mine = jnp.where(core == 0, grads[0], grads[1])
    other = lax.ppermute(jnp.where(core == 0, grads[1], grads[0]), "core", swap)
    half = (mine.astype(F32) + other.astype(F32)).astype(BF16)
    parts = exchange(half, PLANE).reshape(16, CHUNK, 128)
    part = jnp.sum(parts.astype(F32), axis=0).astype(BF16)
    parts = to_all(part, "z", 8).reshape(8, CHUNK, 128)
    part = jnp.sum(parts.astype(F32), axis=0).astype(BF16)
    mine = to_all(part, PLANE, 16)
    other = lax.ppermute(mine, "core", swap)
    left = jnp.where(core == 0, mine, other)
    right = jnp.where(core == 0, other, mine)
    full = jnp.concatenate([left, right], axis=1).astype(F32)
    return (
        encoded.reshape(1, FR // 2, 4, 4, 4 * C),
        full[: 18 * C].reshape(2, 3, 3, C, C),
        full[18 * C : 24 * C].reshape(2, 3, C, C),
        full[24 * C : ROWS].reshape(3, C, C),
        full[ROWS : ROWS + 2],
    )


def solution(mesh):
    fine = Mesh(mesh.devices.reshape(2, 4, 2, 8, 2), EVERY)
    split = P(("xh", "y", "core"), ("z", "xl"), None, None, None)
    return jax.shard_map(
        on_device,
        mesh=fine,
        in_specs=(split, split, P(), P(), P(), P()),
        out_specs=(split, P(), P(), P(), P()),
        check_vma=False,
    )
```

time: 373 us -> 161 us (0.43)
  waiting for transfers between devices: 190 us -> 8.92 us
  matrix products: 37.6 us -> 0 us
  Pallas kernels: 0 us -> 29.8 us
  between operations: 15.1 us -> 0.74 us
  local copies, waits for them, and re-layouts: 18.2 us -> 8.95 us
  blocking collectives: 84.4 us -> 90.5 us
  starting transfers between devices: 18.8 us -> 13.3 us
    psum x1 -> x0, waiting for transfers between devices: 190 us -> none  [on_device(): lax.psum((local_grads[0], local_grads[1], local_grads[2], local_grads[3])...]
    all_to_all x0 -> x3, blocking collectives: none -> 90.5 us  [exchange(): return lax.all_to_all(value, axes, split_axis=0, concat_axis=0, tiled=True)]
    psum x1 -> x0, blocking collectives: 84.4 us -> none  [on_device(): lax.psum((local_grads[0], local_grads[1], local_grads[2], local_grads[3])...]
    dot_general x81 -> x0, matrix products: 37.6 us -> none  [the longest x27 10.9 us: outer_sum(): lax.dot_general(left.reshape(-1, left.shape[-1]), right.reshape(-1, right...]
    pallas_call x0 -> x1, Pallas kernels: none -> 29.8 us  [run_model(): pl.pallas_call(model_kernel, out_shape=(jax.ShapeDtypeStruct((128, 4 * C)...]
    unnamed x37 -> x10, local copies, waits for them, and re-layouts: 10.2 us -> 0.72 us
    ppermute x6 -> x5, waiting for transfers between devices: 0.02 us -> 8.92 us  [the longest x1 3.41 us: on_device(): other = lax.ppermute(jnp.where(core == 0, grads[1], grads[0]), 'core', swap)]
    another operation x13 -> x0, other arithmetic: 5.7 us -> none  [the longest x3 2.92 us: on_device(): jnp.stack(list_sp[::-1])]
  transfers between devices with their start and end apart: 7 -> 5, of which waited for: 1 -> 3; matrix products, arithmetic and copies ran while one was open for 12% -> 3% of each run, Pallas kernels for 0% -> 0%
where the time goes in v1:
time: 161 us
  blocking collectives  90.5 us (56%)
  Pallas kernels  29.8 us (19%)
  starting transfers between devices  13.3 us (8%)
  local copies, waits for them, and re-layouts  8.95 us (6%)
  waiting for transfers between devices  8.92 us (6%)
  other arithmetic  8.45 us (5%)
    all_to_all x3, blocking collectives, exchange(): return lax.all_to_all(value, axes, split_axis=0, concat_axis=0, tiled=True)  90.5 us
    pallas_call x1, Pallas kernels, run_model(): pl.pallas_call(model_kernel, out_shape=(jax.ShapeDtypeStruct((128, 4 * C)...  29.8 us
    ppermute x3, starting transfers between devices, passed_along(): lax.ppermute(value, axes, [(source, source + steps) for source in range(f...  6.53 us
    ppermute x1, starting transfers between devices, on_device(): other = lax.ppermute(mine, 'core', swap)  4.56 us
    ppermute x1, waiting for transfers between devices, on_device(): other = lax.ppermute(jnp.where(core == 0, grads[1], grads[0]), 'core', swap)  3.41 us
  transfers between devices with their start and end apart: 5, of which 3 were waited for; matrix products, arithmetic and copies ran while one was open for 3% of the time, Pallas kernels for 0%

profile of v1, /device:TPU:1, one launch (start us, length us, event | category | flops | bytes accessed | tf_op | source)
XLA Modules:
  0.0 160.7 jit_solution(9849578359936318690)
XLA Ops:
  0.6 0.9 slice.38
  1.6 4.0 %collective-permute-start = (bf16[384,256]{1,0:T(8,128)(2,1)S(1)}, bf16[384,256]{1,0:T(8,128)(2,1)S(1)}, u32[]{:S(2)}, u32[]{:S(2)}) collective-permute-start(bf16[384,256]{1,0:T(8,128)(2,1)S(1)} %bitcast.21), channel_id=1, source_target_pairs={{0,1},{1,2},{2,3},{3,4},{4,5},{5,6},{6,7},{7,8},{8,9},{9,10},{10,1... | collective-permute-start | bytes 589832 | tf_op jit(solution)/shard_map/ppermute | solution.py:303
  5.5 0.9 slice.42
  6.5 1.3 collective-permute-start.2
  7.8 0.8 slice.40
  8.7 1.3 collective-permute-start.1
  9.9 1.7 %reshape.57.cot_ref = bf16[128,1024]{1,0:T(8,128)(2,1)} reshape(bf16[1,8,4,4,1024]{4,3,2,1,0:T(4,128)(2,1)} %param.7) | data formatting | bytes 524288 | tf_op jit(solution)/shard_map/reshape | solution.py:319
  11.7 2.8 %collective-permute-done.1.after_ref = bf16[128,256]{1,0:T(8,128)(2,1)S(1)} collective-permute-done((bf16[128,256]{1,0:T(8,128)(2,1)S(1)}, bf16[128,256]{1,0:T(8,128)(2,1)S(1)}, u32[]{:S(2)}, u32[]{:S(2)}) %collective-permute-start.1) | collective-permute-done | bytes 65568 | tf_op jit(solution)/shard_map/ppermute | solution.py:303
  14.4 0.0 copy-start.4
  14.4 0.0 collective-permute-done.2.cot_after_ref
  14.4 0.0 copy-start.3
  14.4 0.0 collective-permute-done.before_ref
  14.4 0.0 copy-start.2
  14.5 0.6 copy-done.4
  15.1 0.1 copy-done.3
  15.1 0.0 copy-done.2
  15.2 29.8 %shard_map.101 = (bf16[128,1024]{1,0:T(8,128)(2,1)}, bf16[2,7168,128]{2,1,0:T(8,128)(2,1)}) custom-call(bf16[1024,256]{1,0:T(8,128)(2,1)} %bitcast.22, bf16[384,256]{1,0:T(8,128)(2,1)} %copy-done.2, bf16[128,256]{1,0:T(8,128)(2,1)} %copy-done.4, bf16[128,1024]{1,0:T(8,128)(2,1)} %reshape.57.cot_ref, bf16[48,1024]{1,0:T(8,128)(2,1)} %copy-done.3, ...), custom_call_target="tpu_custom_call" | custom-call | flops 12000000000 | bytes 10000000 | tf_op jit(solution)/shard_map/pallas_call | solution.py:267
  44.9 0.0 copy-start
  44.9 2.4 %select_bitcast_fusion = bf16[7168,128]{1,0:T(8,128)(2,1)S(1)} fusion(pred[]{:T(512)S(6)} %eq.2, bf16[2,7168,128]{2,1,0:T(8,128)(2,1)} %get-tuple-element.8), kind=kLoop, calls=%fused_computation.3 | loop fusion | flops 917504 | bytes 5505025 | tf_op jit(solution)/shard_map/jit(_where)/select_n | solution.py:337
  47.3 2.2 %collective-permute-start.3 = (bf16[7168,128]{1,0:T(8,128)(2,1)S(1)}, bf16[7168,128]{1,0:T(8,128)(2,1)S(1)}, u32[]{:S(2)}, u32[]{:S(2)}) collective-permute-start(bf16[7168,128]{1,0:T(8,128)(2,1)S(1)} %select_bitcast_fusion), channel_id=1, source_target_pairs={{0,16},{16,0},{1,17},{17,1},{2,18},{18,2},{3,19},{19,3},{4,20},{20... | collective-permute-start | bytes 5505032 | tf_op jit(solution)/shard_map/ppermute | solution.py:337
  49.6 3.4 %collective-permute-done.3 = bf16[7168,128]{1,0:T(8,128)(2,1)S(1)} collective-permute-done((bf16[7168,128]{1,0:T(8,128)(2,1)S(1)}, bf16[7168,128]{1,0:T(8,128)(2,1)S(1)}, u32[]{:S(2)}, u32[]{:S(2)}) %collective-permute-start.3) | collective-permute-done | bytes 1835040 | tf_op jit(solution)/shard_map/ppermute | solution.py:337
  53.0 0.0 copy-done
  53.0 0.7 fusion
  53.7 32.4 %all_to_all.24 = bf16[16,448,128]{2,1,0:T(8,128)(2,1)S(1)} all-to-all(bf16[16,448,128]{2,1,0:T(8,128)(2,1)S(1)} %bitcast.17), channel_id=1, replica_groups=mesh['xh'=2,'y'=4,'core'=2,'z'=8,'xl'=2] {'xh','xl','y'}, dimensions={0} | all-to-all | bytes 3670016 | tf_op jit(solution)/shard_map/all_to_all | solution.py:307
  86.1 0.3 reduce_sum.24
  86.3 0.1 broadcast_in_dim.4
  86.5 32.3 %all_to_all.25 = bf16[8,448,128]{2,1,0:T(8,128)(2,1)S(1)} all-to-all(bf16[8,448,128]{2,1,0:T(8,128)(2,1)S(1)} %broadcast_in_dim.4), channel_id=1, replica_groups=mesh['xh'=2,'y'=4,'core'=2,'z'=8,'xl'=2] {'z'}, dimensions={0} | all-to-all | bytes 1835008 | tf_op jit(solution)/shard_map/all_to_all | solution.py:307
  118.7 0.1 reduce_sum.25
  118.9 0.3 broadcast_in_dim.5
  119.2 0.0 copy-start.1
  119.2 25.8 %all_to_all.26 = bf16[16,448,128]{2,1,0:T(8,128)(2,1)S(1)} all-to-all(bf16[16,448,128]{2,1,0:T(8,128)(2,1)S(1)} %broadcast_in_dim.5), channel_id=1, replica_groups=mesh['xh'=2,'y'=4,'core'=2,'z'=8,'xl'=2] {'xh','xl','y'}, dimensions={0} | all-to-all | bytes 3670016 | tf_op jit(solution)/shard_map/all_to_all | solution.py:307
  145.1 4.6 %collective-permute-start.4 = (bf16[7168,128]{1,0:T(8,128)(2,1)S(1)}, bf16[7168,128]{1,0:T(8,128)(2,1)}, u32[]{:S(2)}, u32[]{:S(2)}) collective-permute-start(bf16[7168,128]{1,0:T(8,128)(2,1)S(1)} %bitcast.16), channel_id=1, source_target_pairs={{0,16},{16,0},{1,17},{17,1},{2,18},{18,2},{3,19},{19,3},{4,20},{20... | collective-permute-start | bytes 5505032 | tf_op jit(solution)/shard_map/ppermute | solution.py:344
  149.6 0.0 copy-done.1
  149.6 0.8 reshape.59
  150.5 2.7 %collective-permute-done.4 = bf16[7168,128]{1,0:T(8,128)(2,1)} collective-permute-done((bf16[7168,128]{1,0:T(8,128)(2,1)S(1)}, bf16[7168,128]{1,0:T(8,128)(2,1)}, u32[]{:S(2)}, u32[]{:S(2)}) %collective-permute-start.4) | collective-permute-done | bytes 1835040 | tf_op jit(solution)/shard_map/ppermute | solution.py:344
  153.2 1.7 %broadcast_select_fusion.1 = (bf16[7168,128]{1,0:T(8,128)(2,1)S(1)}, bf16[7168,128]{1,0:T(8,128)(2,1)S(1)}) fusion(bf16[7168,128]{1,0:T(8,128)(2,1)} %collective-permute-done.4, pred[]{:T(512)S(6)} %eq.2, bf16[16,448,128]{2,1,0:T(8,128)(2,1)S(1)} %all_to_all.26), kind=kLoop, calls=%fused_computation.5 | loop fusion | flops 1835008 | bytes 7340033 | tf_op jit(solution)/shard_map/jit(_where)/select_n | solution.py:345
  154.9 0.6 maximum_convert_fusion.3
  155.5 0.9 maximum_convert_fusion.2
  156.4 1.2 maximum_convert_fusion.1
  157.7 0.5 maximum_convert_fusion
  158.2 2.5 %slice.50 = f32[4608,256]{1,0:T(8,128)} slice(f32[7168,256]{1,0:T(8,128)S(1)} %maximum_convert_fusion), slice={[0:4608], [0:256]} | slice | bytes 9437184 | tf_op jit(solution)/shard_map/slice | solution.py:350
  (1 shorter events, 0.0 us)
Async XLA Ops:
  1.6 12.9 %collective-permute-start = (bf16[384,256]{1,0:T(8,128)(2,1)S(1)}, bf16[384,256]{1,0:T(8,128)(2,1)S(1)}, u32[]{:S(2)}, u32[]{:S(2)}) collective-permute-start(bf16[384,256]{1,0:T(8,128)(2,1)S(1)} %bitcast.21), channel_id=1, source_target_pairs={{0,1},{1,2},{2,3},{3,4},{4,5},{5,6},{6,7},{7,8},{8,9},{9,10},{10,1... | collective-permute-start | bytes 589832 | tf_op jit(solution)/shard_map/ppermute | solution.py:303
  6.5 7.9 %collective-permute-start.2 = (bf16[48,1024]{1,0:T(8,128)(2,1)S(1)}, bf16[48,1024]{1,0:T(8,128)(2,1)S(1)}, u32[]{:S(2)}, u32[]{:S(2)}) collective-permute-start(bf16[48,1024]{1,0:T(8,128)(2,1)S(1)} %slice.43), channel_id=1, source_target_pairs={{1,0},{2,1},{3,2},{4,3},{5,4},{6,5},{7,6},{8,7},{9,8},{10,9},{11,1... | collective-permute-start | bytes 294920 | tf_op jit(solution)/shard_map/ppermute | solution.py:303
  8.7 5.8 %collective-permute-start.1 = (bf16[128,256]{1,0:T(8,128)(2,1)S(1)}, bf16[128,256]{1,0:T(8,128)(2,1)S(1)}, u32[]{:S(2)}, u32[]{:S(2)}) collective-permute-start(bf16[128,256]{1,0:T(8,128)(2,1)S(1)} %bitcast.23), channel_id=1, source_target_pairs={{1,0},{2,1},{3,2},{4,3},{5,4},{6,5},{7,6},{8,7},{9,8},{10,9},{11,1... | collective-permute-start | bytes 196616 | tf_op jit(solution)/shard_map/ppermute | solution.py:303
  14.4 0.6 copy-start.4
  14.4 0.7 copy-start.3
  14.4 0.7 copy-start.2
  44.9 8.0 %copy-start = (bf16[2,7168,128]{2,1,0:T(8,128)(2,1)S(1)}, bf16[2,7168,128]{2,1,0:T(8,128)(2,1)}, u32[]{:S(2)}) copy-start(bf16[2,7168,128]{2,1,0:T(8,128)(2,1)} %get-tuple-element.8) | copy-start | bytes 11010052
  47.3 5.6 %collective-permute-start.3 = (bf16[7168,128]{1,0:T(8,128)(2,1)S(1)}, bf16[7168,128]{1,0:T(8,128)(2,1)S(1)}, u32[]{:S(2)}, u32[]{:S(2)}) collective-permute-start(bf16[7168,128]{1,0:T(8,128)(2,1)S(1)} %select_bitcast_fusion), channel_id=1, source_target_pairs={{0,16},{16,0},{1,17},{17,1},{2,18},{18,2},{3,19},{19,3},{4,20},{20... | collective-permute-start | bytes 5505032 | tf_op jit(solution)/shard_map/ppermute | solution.py:337
  119.2 30.4 %copy-start.1 = (bf16[128,1024]{1,0:T(8,128)(2,1)S(1)}, bf16[128,1024]{1,0:T(8,128)(2,1)}, u32[]{:S(2)}) copy-start(bf16[128,1024]{1,0:T(8,128)(2,1)} %get-tuple-element.7) | copy-start | bytes 786436
  145.1 8.1 %collective-permute-start.4 = (bf16[7168,128]{1,0:T(8,128)(2,1)S(1)}, bf16[7168,128]{1,0:T(8,128)(2,1)}, u32[]{:S(2)}, u32[]{:S(2)}) collective-permute-start(bf16[7168,128]{1,0:T(8,128)(2,1)S(1)} %bitcast.16), channel_id=1, source_target_pairs={{0,16},{16,0},{1,17},{17,1},{2,18},{18,2},{3,19},{19,3},{4,20},{20... | collective-permute-start | bytes 5505032 | tf_op jit(solution)/shard_map/ppermute | solution.py:344

commit v2 on v1

v2 whole, which is shorter than its diff:
```python
import jax
import jax.numpy as jnp
from jax import lax
from jax.experimental import pallas as pl
from jax.experimental.pallas import tpu as pltpu
from jax.sharding import Mesh, PartitionSpec as P

EPSILON = 1e-06
F32 = jnp.float32
BF16 = jnp.bfloat16
C = 256
PIX = 64
FR = 16
UNROLL = 2
OUT = pltpu.VMEM
HBM = pltpu.HBM
MATS = 27
ROWS = MATS * C
CHUNK = 448
FLAT = 16 * CHUNK
EVERY = ("xh", "y", "core", "z", "xl")
PLANE = ("xh", "xl", "y")


def dot(left, right):
    return jnp.dot(left, right, preferred_element_type=F32)


def dot_nt(left, right):
    return lax.dot_general(left, right, (((1,), (1,)), ((), ())), preferred_element_type=F32)


def dot_tn(left, right):
    return lax.dot_general(left, right, (((0,), (0,)), ((), ())), preferred_element_type=F32)


def frames(first, count):
    return pl.ds(first * PIX, count * PIX)


def one_frame(index):
    return pl.ds(pl.multiple_of(index * PIX, PIX), PIX)


def write_windows(value, im_ref, rows, sign):
    grid = value.reshape(8, 8, C)
    column = lax.broadcasted_iota(jnp.int32, (8, 8, C), 1)
    blank = jnp.zeros((1, 8, C), F32)
    for j in range(3):
        dx = sign * (j - 1)
        if dx == 0:
            moved = grid
        elif dx == 1:
            moved = jnp.where(column == 7, 0.0, pltpu.roll(grid, 7, 1))
        else:
            moved = jnp.where(column == 0, 0.0, pltpu.roll(grid, 1, 1))
        for i in range(3):
            dy = sign * (i - 1)
            if dy == 0:
                placed = moved
            elif dy == 1:
                placed = jnp.concatenate([moved[1:], blank], axis=0)
            else:
                placed = jnp.concatenate([blank, moved[:-1]], axis=0)
            tap = 3 * i + j
            im_ref[rows, tap * C : (tap + 1) * C] = placed.reshape(PIX, C).astype(BF16)


def place_matrix(groups):
    size = groups * 8
    dest = lax.broadcasted_iota(jnp.int32, (size, size), 0)
    src = lax.broadcasted_iota(jnp.int32, (size, size), 1)
    want = (dest & 1) * (groups * 4) + (dest >> 3) * 4 + ((dest >> 1) & 3)
    return jnp.where(src == want, 1.0, 0.0).astype(BF16)


def ungroup(piece, groups, one_hot):
    halves = []
    for i in range(2):
        both = jnp.concatenate([piece(2 * i + j) for j in range(2)], axis=0)
        halves.append(dot(one_hot, both).reshape(groups, 8, C))
    return jnp.concatenate(halves, axis=1).reshape(groups * 16, C).astype(BF16)


def norm_windows(src, first, count, gain, im, n_ref=None):
    def body(index, _):
        rows = one_frame(index)
        value = src[one_frame(index + first), :].astype(F32)
        inv = lax.rsqrt(jnp.mean(value * value, axis=-1, keepdims=True) + EPSILON)
        value = value * inv * gain
        write_windows(value, im, rows, 1)
        if n_ref is not None:
            n_ref[rows, :] = value.astype(BF16)
        return 0

    lax.fori_loop(0, count, body, 0, unroll=UNROLL)


def activate(im, weights, pieces, act, slope):
    for first, size, act_first, slope_first in pieces:
        conv = dot(im[pl.ds(first, size), :], weights.reshape(9 * C, C))
        logistic = jax.nn.sigmoid(conv)
        act[pl.ds(act_first, size), :] = (conv * logistic).astype(BF16)
        if slope_first is not None:
            slope[pl.ds(slope_first, size), :] = logistic * (1.0 + conv * (1.0 - logistic))


def front_kernel(
    video_hbm, gains_hbm, sw_hbm, n_ref, act_ref, slope_ref, im, video, gains, weights, sems
):
    copies = [
        pltpu.make_async_copy(video_hbm, video, sems.at[0]),
        pltpu.make_async_copy(gains_hbm, gains, sems.at[1]),
        pltpu.make_async_copy(sw_hbm.at[0], weights, sems.at[2]),
    ]
    for copy in copies:
        copy.start()
    copies[0].wait()
    copies[1].wait()
    norm_windows(video, 0, FR, gains[0:1, :], im, n_ref)
    copies[2].wait()
    activate(im, weights[...], [(0, 512, 0, 0), (512, 512, 512, 512)], act_ref, slope_ref)


def model_kernel(
    core_ref,
    n1_ref,
    a1_ref,
    slope1,
    before_ref,
    after_ref,
    cot_ref,
    video_hbm,
    gains_hbm,
    sw_hbm,
    tw_hbm,
    rw_hbm,
    enc_ref,
    mine_ref,
    theirs_ref,
    s1,
    s2,
    im,
    n2_ref,
    a1,
    a2,
    slope2,
    low,
    cotf,
    up,
    g2,
    g1,
    ga,
    gn,
    wcat,
    video,
    gains_ref,
    sw_ref,
    tw_ref,
    rw_ref,
    sems,
):
    pairs = [
        (gains_hbm, gains_ref),
        (sw_hbm.at[0], sw_ref.at[0]),
        (video_hbm, video),
        (tw_hbm, tw_ref),
        (sw_hbm.at[1], sw_ref.at[1]),
        (rw_hbm, rw_ref),
    ]
    copies = [pltpu.make_async_copy(*pair, sems.at[i]) for i, pair in enumerate(pairs)]
    for copy in copies:
        copy.start()
    s1[frames(0, 6), :] = before_ref[...].astype(F32)
    s1[frames(22, 2), :] = after_ref[: 2 * PIX].astype(F32)
    a1[frames(6, 16), :] = a1_ref[...]
    n_refs = (n1_ref, n2_ref)
    first_core = core_ref[0] == 0

    def put_halves(rows, value):
        low_half = value[:, :128].astype(BF16)
        high_half = value[:, 128:].astype(BF16)
        mine_ref[rows, :] = jnp.where(first_core, low_half, high_half)
        theirs_ref[rows, :] = jnp.where(first_core, high_half, low_half)

    def put(matrix, value):
        put_halves(pl.ds(matrix * C, C), value)

    def temporal(act, first, count, block):
        with_edge = jnp.concatenate([act[frames(first - k, count), :] for k in range(3)], axis=1)
        return dot(with_edge, tw_ref[block].reshape(3 * C, C))

    copies[0].wait()
    norm_windows(s1, 0, 6, gains_ref[0:1, :], im)
    norm_windows(s1, 22, 2, gains_ref[0:1, :], im.at[frames(6, 2)])
    copies[1].wait()
    activate(im, sw_ref[0], [(0, 384, 0, None), (384, 128, 1408, None)], a1, None)
    copies[2].wait()
    s1[frames(6, 16), :] = video[...].astype(F32)
    copies[3].wait()
    for first, count in ((0, 11), (11, 10)):
        s2[frames(first, count), :] = s1[frames(first + 3, count), :] + temporal(
            a1, first + 3, count, 0
        )
    norm_windows(s2, 0, 3, gains_ref[1:2, :], im)
    norm_windows(s2, 3, 16, gains_ref[1:2, :], im.at[frames(3, 16)], n2_ref)
    norm_windows(s2, 19, 2, gains_ref[1:2, :], im.at[frames(19, 2)])
    copies[4].wait()
    activate(im, sw_ref[1], [(0, 672, 0, 0), (672, 672, 672, 672)], a2, slope2)
    copies[5].wait()
    low[frames(0, 17), :] = (s2[frames(2, 17), :] + temporal(a2, 2, 17, 1)).astype(BF16)
    low[frames(17, 1), :] = jnp.zeros((PIX, C), BF16)

    pairs = low[...].reshape(9, 2 * PIX, C)
    taps = jnp.concatenate(
        [
            pairs[1:9, :PIX].reshape(8 * PIX, C),
            pairs[0:8, PIX:].reshape(8 * PIX, C),
            pairs[0:8, :PIX].reshape(8 * PIX, C),
        ],
        axis=1,
    )
    one_hot = place_matrix(32)
    down = dot(taps, rw_ref[...].reshape(3 * C, C)).astype(BF16).astype(F32)
    down = down.reshape(32, 16, C)
    for i in range(2):
        both = dot_tn(one_hot, down[:, i * 8 : (i + 1) * 8].reshape(256, C).astype(BF16))
        for j in range(2):
            tap = 2 * i + j
            enc_ref[:, tap * C : (tap + 1) * C] = both[j * 128 : (j + 1) * 128].astype(BF16)
    cotf[frames(0, 8), :] = ungroup(
        lambda tap: cot_ref[:, tap * C : (tap + 1) * C], 32, one_hot
    )
    cotf[frames(8, 3), :] = ungroup(
        lambda tap: after_ref[2 * PIX + tap * 48 : 2 * PIX + (tap + 1) * 48, :],
        12,
        place_matrix(12),
    )
    grad_down = dot_tn(taps, cotf[frames(0, 8), :])
    for k in range(3):
        put(24 + k, grad_down[k * C : (k + 1) * C])
    even = dot_nt(cotf[frames(0, 10), :], rw_ref[1])
    odd = dot_nt(cotf[frames(0, 10), :], rw_ref[0]) + dot_nt(cotf[frames(1, 10), :], rw_ref[2])
    merged = jnp.concatenate(
        [even.reshape(10, PIX, C), odd.reshape(10, PIX, C)], axis=1
    ).reshape(20 * PIX, C)
    up[...] = merged[: 18 * PIX]
    g2[...] = merged.astype(BF16)

    def block_back(block, grad, act, own, slope, slope_own, count, pieces):
        with_edge = jnp.concatenate([act[frames(own - k, FR), :] for k in range(3)], axis=1)
        grad_time = dot_tn(with_edge, grad[frames(0, FR), :])
        for k in range(3):
            put(18 + 3 * block + k, grad_time[k * C : (k + 1) * C])
        for k in range(3):
            wcat[:, k * C : (k + 1) * C] = tw_ref[block, k]
        for first, size in pieces:
            later = jnp.concatenate(
                [grad[pl.ds(first + k * PIX, size), :] for k in range(3)], axis=1
            )
            ga[pl.ds(first, size), :] = dot_nt(later, wcat[:, : 3 * C])

        def body(index, _):
            rows = one_frame(index)
            write_windows(ga[rows, :] * slope[one_frame(index + slope_own), :], im, rows, -1)
            return 0

        lax.fori_loop(0, count, body, 0, unroll=UNROLL)
        for tap in range(9):
            wcat[:, tap * C : (tap + 1) * C] = sw_ref[block, tap]
        for first, size in pieces:
            gn[pl.ds(first, size), :] = dot_nt(im[pl.ds(first, size), :], wcat[...])
        for i in range(3):
            grad_sp = dot_tn(n_refs[block][...], im[frames(0, FR), 3 * i * C : 3 * (i + 1) * C])
            for j in range(3):
                put(9 * block + 3 * i + j, grad_sp[:, j * C : (j + 1) * C])

    def gain_part(index, src, own):
        value = src[one_frame(index + own), :]
        inv = lax.rsqrt(jnp.mean(value * value, axis=-1, keepdims=True) + EPSILON)
        unit = value * inv
        grad = gn[one_frame(index), :]
        return grad, unit, inv

    block_back(1, g2, a2, 3, slope2, 3, 18, [(0, 576), (576, 576)])
    gain = gains_ref[1:2, :]

    def norm_back(index, total):
        grad, unit, inv = gain_part(index, s2, 3)
        scaled = grad * gain
        back = inv * (scaled - unit * jnp.mean(unit * scaled, axis=-1, keepdims=True))
        rows = one_frame(index)
        g1[rows, :] = (up[rows, :] + back).astype(BF16)
        return total + jnp.sum((grad * unit).reshape(8, 8, C), axis=0)

    none = jnp.zeros((8, C), F32)
    total2 = lax.fori_loop(0, FR, norm_back, none, unroll=UNROLL)
    lax.fori_loop(FR, FR + 2, norm_back, none)

    block_back(0, g1, a1, 6, slope1, 0, 16, [(0, 512), (512, 512)])

    def gain_only(index, total):
        grad, unit, _ = gain_part(index, s1, 6)
        return total + jnp.sum((grad * unit).reshape(8, 8, C), axis=0)

    total1 = lax.fori_loop(0, FR, gain_only, none, unroll=UNROLL)
    rest = jnp.concatenate(
        [
            jnp.sum(total1, axis=0, keepdims=True),
            jnp.sum(total2, axis=0, keepdims=True),
            jnp.zeros((14, C), F32),
        ],
        axis=0,
    )
    put_halves(pl.ds(ROWS, 16), rest)
    for ref in (mine_ref, theirs_ref):
        ref[ROWS + 16 :, :] = jnp.zeros((FLAT - ROWS - 16, 128), BF16)


def run_model(core, video, before, after, cot, gains, sw, tw, rw):
    def vm(rows, dtype, cols=C):
        return pltpu.VMEM((rows * PIX, cols), dtype)

    whole = pl.BlockSpec(memory_space=pltpu.VMEM)
    hbm = pl.BlockSpec(memory_space=HBM)
    normed, act, slope = pl.pallas_call(
        front_kernel,
        out_shape=(OUT((FR * PIX, C), BF16), OUT((FR * PIX, C), BF16), OUT((FR * PIX, C), F32)),
        in_specs=[hbm] * 3,
        out_specs=(whole,) * 3,
        scratch_shapes=[
            vm(16, BF16, 9 * C),
            vm(16, BF16),
            pltpu.VMEM((2, C), F32),
            pltpu.VMEM((9, C, C), BF16),
            pltpu.SemaphoreType.DMA((3,)),
        ],
        compiler_params=pltpu.CompilerParams(vmem_limit_bytes=24 * 1024 * 1024),
        cost_estimate=pl.CostEstimate(
            flops=1_200_000_000, bytes_accessed=4_000_000, transcendentals=500_000
        ),
    )(video, gains, sw)
    return pl.pallas_call(
        model_kernel,
        out_shape=(
            jax.ShapeDtypeStruct((128, 4 * C), BF16),
            OUT((FLAT, 128), BF16),
            OUT((FLAT, 128), BF16),
        ),
        in_specs=[pl.BlockSpec(memory_space=pltpu.SMEM)] + [whole] * 6 + [hbm] * 5,
        out_specs=(whole, whole, whole),
        scratch_shapes=[
            vm(24, F32),
            vm(21, F32),
            vm(21, BF16, 9 * C),
            vm(16, BF16),
            vm(24, BF16),
            vm(21, BF16),
            vm(21, F32),
            vm(18, BF16),
            vm(11, BF16),
            vm(18, F32),
            vm(20, BF16),
            vm(18, BF16),
            vm(18, F32),
            vm(18, F32),
            pltpu.VMEM((C, 9 * C), BF16),
            vm(16, BF16),
            pltpu.VMEM((2, C), F32),
            pltpu.VMEM((2, 9, C, C), BF16),
            pltpu.VMEM((2, 3, C, C), BF16),
            pltpu.VMEM((3, C, C), BF16),
            pltpu.SemaphoreType.DMA((6,)),
        ],
        compiler_params=pltpu.CompilerParams(vmem_limit_bytes=40 * 1024 * 1024),
        cost_estimate=pl.CostEstimate(
            flops=10_000_000_000, bytes_accessed=8_000_000, transcendentals=1_000_000
        ),
    )(core, normed, act, slope, before, after, cot, video, gains, sw, tw, rw)


def passed_along(value, axes, steps):
    count = lax.axis_size(axes)
    first, last = (max(0, -steps), min(count, count - steps))
    return lax.ppermute(value, axes, [(source, source + steps) for source in range(first, last)])


def exchange(value, axes):
    return lax.all_to_all(value, axes, split_axis=0, concat_axis=0, tiled=True)


def to_all(value, axes, count):
    rows, cols = value.shape
    copies = jnp.broadcast_to(value[None], (count, rows, cols)).reshape(count * rows, cols)
    return exchange(copies, axes)


def place_kernel(core_ref, part_ref, *refs):
    sp_ref, tm_ref, dn_ref, gn_ref, buf, gains, sems = refs[-7:]
    lanes = pl.ds(pl.multiple_of(core_ref[0] * 128, 128), 128)
    copies = []
    for matrix in range(MATS):
        buf[matrix] = part_ref[pl.ds(matrix * C, C), :].astype(F32)
        if matrix < 18:
            target = sp_ref.at[matrix, :, lanes]
        elif matrix < 24:
            target = tm_ref.at[matrix - 18, :, lanes]
        else:
            target = dn_ref.at[matrix - 24, :, lanes]
        copies.append(pltpu.make_async_copy(buf.at[matrix], target, sems.at[matrix]))
        copies[-1].start()
    gains[...] = part_ref[ROWS : ROWS + 16, :].astype(F32)[:8]
    copies.append(pltpu.make_async_copy(gains, gn_ref.at[:, lanes], sems.at[MATS]))
    copies[-1].start()
    for copy in copies:
        copy.wait()


def place(which, part, outputs=()):
    whole = pl.BlockSpec(memory_space=pltpu.VMEM)
    hbm = pl.BlockSpec(memory_space=HBM)
    return pl.pallas_call(
        place_kernel,
        out_shape=(
            jax.ShapeDtypeStruct((18, C, C), F32),
            jax.ShapeDtypeStruct((6, C, C), F32),
            jax.ShapeDtypeStruct((3, C, C), F32),
            jax.ShapeDtypeStruct((8, C), F32),
        ),
        in_specs=[pl.BlockSpec(memory_space=pltpu.SMEM), whole] + [hbm] * len(outputs),
        out_specs=(hbm,) * 4,
        scratch_shapes=[
            pltpu.VMEM((MATS, C, 128), F32),
            pltpu.VMEM((8, 128), F32),
            pltpu.SemaphoreType.DMA((MATS + 1,)),
        ],
        input_output_aliases={2 + i: i for i in range(len(outputs))},
        compiler_params=pltpu.CompilerParams(vmem_limit_bytes=16 * 1024 * 1024),
        cost_estimate=pl.CostEstimate(flops=0, bytes_accessed=6_000_000, transcendentals=0),
    )(which, part, *outputs)


def on_device(video, cotangent, gains, spatial_weights, time_weights, reduce_kernel_weights):
    tm = ("z", "xl")
    video = video.reshape(FR * PIX, C)
    cot = cotangent.reshape(FR * 8, 4 * C)
    before = passed_along(video[-6 * PIX :], tm, 1)
    leading = [video[: 2 * PIX]] + [cot[:48, tap * C : (tap + 1) * C] for tap in range(4)]
    after = passed_along(jnp.concatenate(leading, axis=0), tm, -1)
    core = lax.axis_index("core").astype(jnp.int32).reshape(1)
    encoded, mine, theirs = run_model(
        core,
        video,
        before,
        after,
        cot,
        gains,
        spatial_weights.reshape(2, 9, C, C),
        time_weights,
        reduce_kernel_weights,
    )
    swap = [(0, 1), (1, 0)]
    other = lax.ppermute(theirs, "core", swap)
    half = (mine.astype(F32) + other.astype(F32)).astype(BF16)
    parts = exchange(half, PLANE).reshape(16, CHUNK, 128)
    part = jnp.sum(parts.astype(F32), axis=0).astype(BF16)
    parts = exchange(part, "z").reshape(8, CHUNK // 8, 128)
    part = jnp.sum(parts.astype(F32), axis=0).astype(BF16)
    part = to_all(part, "z", 8)
    mine = to_all(part, PLANE, 16)
    other = lax.ppermute(mine, "core", swap)
    outputs = place(core, mine)
    grad_sp, grad_tm, grad_dn, grad_gn = place(1 - core, other, outputs)
    return (
        encoded.reshape(1, FR // 2, 4, 4, 4 * C),
        grad_sp.reshape(2, 3, 3, C, C),
        grad_tm.reshape(2, 3, C, C),
        grad_dn,
        grad_gn[:2],
    )


def solution(mesh):
    fine = Mesh(mesh.devices.reshape(2, 4, 2, 8, 2), EVERY)
    split = P(("xh", "y", "core"), ("z", "xl"), None, None, None)
    return jax.shard_map(
        on_device,
        mesh=fine,
        in_specs=(split, split, P(), P(), P(), P()),
        out_specs=(split, P(), P(), P(), P()),
        check_vma=False,
    )
```

time: 161 us -> 140 us (0.87)
  other arithmetic: 8.45 us -> 0.75 us
  blocking collectives: 90.5 us -> 84.3 us
  waiting for transfers between devices: 8.92 us -> 4.12 us
    pallas_call x1, Pallas kernels: 29.8 us -> 20.7 us  [run_model(): pl.pallas_call(model_kernel, out_shape=(jax.ShapeDtypeStruct((128, 4 * C)...]
    pallas_call x0 -> x3, Pallas kernels: none -> 8.46 us  [the longest x2 5.55 us: place(): pl.pallas_call(place_kernel, out_shape=(jax.ShapeDtypeStruct((18, C, C),...]
    all_to_all x3 -> x4, blocking collectives: 90.5 us -> 84.3 us  [exchange(): return lax.all_to_all(value, axes, split_axis=0, concat_axis=0, tiled=True)]
    select_n x2 -> x0, other arithmetic: 4.13 us -> none  [the longest x1 2.39 us: on_device(): other = lax.ppermute(jnp.where(core == 0, grads[1], grads[0]), 'core', swap)]
    slice x4 -> x2, local copies, waits for them, and re-layouts: 4.3 us -> 1.43 us  [the longest x1 0.85 us: on_device(): video[:2 * PIX]]
    ppermute x3 -> x2, waiting for transfers between devices: 2.77 us -> 0.01 us  [passed_along(): lax.ppermute(value, axes, [(source, source + steps) for source in range(f...]
    slice x3 -> x0, other arithmetic: 2.76 us -> none  [the longest x1 1.24 us: on_device(): full[18 * C:24 * C].reshape(2, 3, C, C)]
    unnamed x10 -> x20, local copies, waits for them, and re-layouts: 0.72 us -> 3.43 us
  transfers between devices with their start and end apart: 5 -> 4, of which waited for: 3 -> 2; matrix products, arithmetic and copies ran while one was open for 3% -> 2% of each run, Pallas kernels for 0% -> 4%
where the time goes in v2:
time: 140 us; the launch traced here: 139 us
  blocking collectives  84.3 us (60%)
  Pallas kernels  29.1 us (21%)
  starting transfers between devices  12.2 us (9%)
  local copies, waits for them, and re-layouts  7.98 us (6%)
  waiting for transfers between devices  4.12 us (3%)
    all_to_all x4, blocking collectives, exchange(): return lax.all_to_all(value, axes, split_axis=0, concat_axis=0, tiled=True)  84.3 us
    pallas_call x1, Pallas kernels, run_model(): pl.pallas_call(model_kernel, out_shape=(jax.ShapeDtypeStruct((128, 4 * C)...  20.7 us
    ppermute x1, starting transfers between devices, on_device(): other = lax.ppermute(mine, 'core', swap)  5.73 us
    pallas_call x2, Pallas kernels, place(): pl.pallas_call(place_kernel, out_shape=(jax.ShapeDtypeStruct((18, C, C),...  5.55 us
    ppermute x2, starting transfers between devices, passed_along(): lax.ppermute(value, axes, [(source, source + steps) for source in range(f...  5.25 us
    unnamed x20, local copies, waits for them, and re-layouts  3.43 us
    ppermute x1, waiting for transfers between devices, on_device(): other = lax.ppermute(theirs, 'core', swap)  3.41 us
    pallas_call x1, Pallas kernels, run_model(): pl.pallas_call(front_kernel, out_shape=(OUT((FR * PIX, C), BF16), OUT((FR...  2.92 us
  transfers between devices with their start and end apart: 4, of which 2 were waited for; matrix products, arithmetic and copies ran while one was open for 2% of the time, Pallas kernels for 4%

profile of v2, /device:TPU:1, one launch (start us, length us, event | category | flops | bytes accessed | tf_op | source)
XLA Modules:
  0.0 139.3 jit_solution(13434615158259232053)
XLA Ops:
  0.6 0.9 slice.27
  1.6 4.0 %collective-permute-start = (bf16[384,256]{1,0:T(8,128)(2,1)S(1)}, bf16[384,256]{1,0:T(8,128)(2,1)S(1)}, u32[]{:S(2)}, u32[]{:S(2)}) collective-permute-start(bf16[384,256]{1,0:T(8,128)(2,1)S(1)} %bitcast.23), channel_id=1, source_target_pairs={{0,1},{1,2},{2,3},{3,4},{4,5},{5,6},{6,7},{7,8},{8,9},{9,10},{10,1... | collective-permute-start | bytes 589832 | tf_op jit(solution)/shard_map/ppermute | solution.py:385
  5.5 0.8 slice.29
  6.4 1.0 reshape.55.cot_ref
  7.5 1.3 collective-permute-start.1
  8.8 0.0 copy-start
  8.8 1.0 copy-done
  9.8 0.0 copy-start.2
  9.8 1.7 %copy-done.2 = bf16[2,3,3,256,256]{4,3,2,1,0:T(8,128)(2,1)S(1)} copy-done((bf16[2,3,3,256,256]{4,3,2,1,0:T(8,128)(2,1)S(1)}, bf16[2,3,3,256,256]{4,3,2,1,0:T(8,128)(2,1)}, u32[]{:S(2)}) %copy-start.2) | copy-done | bytes 2359320
  11.5 0.0 copy-start.6
  11.5 0.7 copy-done.6
  12.2 0.0 copy-start.1
  12.2 0.0 copy-start.3
  12.2 0.0 copy-start.4
  12.2 0.0 copy-start.5
  12.2 0.0 copy-start.7
  12.2 2.9 %shard_map.101 = (bf16[1024,256]{1,0:T(8,128)(2,1)S(1)}, bf16[1024,256]{1,0:T(8,128)(2,1)S(1)}, f32[1024,256]{1,0:T(8,128)S(1)}) custom-call(bf16[1024,256]{1,0:T(8,128)(2,1)S(1)} %bitcast.13, f32[2,256]{1,0:T(2,128)S(1)} %copy-done.6, bf16[2,9,256,256]{3,2,1,0:T(8,128)(2,1)S(1)} %bitcast.15), custom_call_target="tpu_custom_call" | custom-call | flops 1200000000 | bytes 4000000 | tf_op jit(solution)/shard_map/pallas_call | solution.py:326
  15.1 0.0 collective-permute-done.1.after_ref
  15.1 0.0 collective-permute-done.before_ref
  15.1 0.0 copy-done.1
  15.1 0.0 copy-done.3
  15.2 0.0 copy-done.4
  15.2 0.0 copy-done.5
  15.2 0.0 copy-done.7
  15.2 20.7 %shard_map.102 = (bf16[128,1024]{1,0:T(8,128)(2,1)S(1)}, bf16[7168,128]{1,0:T(8,128)(2,1)S(1)}, bf16[7168,128]{1,0:T(8,128)(2,1)S(1)}) custom-call(s32[1]{0:T(128)} %bitcast.core_ref, bf16[1024,256]{1,0:T(8,128)(2,1)S(1)} %get-tuple-element.19.n1_ref, bf16[1024,256]{1,0:T(8,128)(2,1)S(1)} %get-tuple-element.20.a1_ref, ...), custom_call_target="tpu_custom_call" | custom-call | flops 10000000000 | bytes 8000000 | tf_op jit(solution)/shard_map/pallas_call | solution.py:343
  35.8 1.3 collective-permute-start.2
  37.1 3.4 %collective-permute-done.2 = bf16[7168,128]{1,0:T(8,128)(2,1)S(1)} collective-permute-done((bf16[7168,128]{1,0:T(8,128)(2,1)S(1)}, bf16[7168,128]{1,0:T(8,128)(2,1)S(1)}, u32[]{:S(2)}, u32[]{:S(2)}) %collective-permute-start.2) | collective-permute-done | bytes 1835040 | tf_op jit(solution)/shard_map/ppermute | solution.py:463
  40.5 0.5 add_convert_fusion
  41.0 32.2 %all_to_all.32 = bf16[16,448,128]{2,1,0:T(8,128)(2,1)S(1)} all-to-all(bf16[16,448,128]{2,1,0:T(8,128)(2,1)S(1)} %bitcast.17), channel_id=1, replica_groups=mesh['xh'=2,'y'=4,'core'=2,'z'=8,'xl'=2] {'xh','xl','y'}, dimensions={0} | all-to-all | bytes 3670016 | tf_op jit(solution)/shard_map/all_to_all | solution.py:389
  73.2 0.3 reduce_sum.24
  73.5 17.9 %all_to_all.33 = bf16[8,56,128]{2,1,0:T(8,128)(2,1)S(1)} all-to-all(bf16[8,56,128]{2,1,0:T(8,128)(2,1)S(1)} %bitcast.20), channel_id=1, replica_groups=mesh['xh'=2,'y'=4,'core'=2,'z'=8,'xl'=2] {'z'}, dimensions={0} | all-to-all | bytes 229376 | tf_op jit(solution)/shard_map/all_to_all | solution.py:389
  91.4 10.2 %all_to_all.34 = bf16[8,56,128]{2,1,0:T(8,128)(2,1)S(1)} all-to-all(bf16[8,56,128]{2,1,0:T(8,128)(2,1)S(1)} %broadcast_in_dim.6), channel_id=1, replica_groups=mesh['xh'=2,'y'=4,'core'=2,'z'=8,'xl'=2] {'z'}, dimensions={0} | all-to-all | bytes 229376 | tf_op jit(solution)/shard_map/all_to_all | solution.py:389
  101.7 0.3 broadcast_in_dim.16
  102.0 23.9 %all_to_all.35 = bf16[16,448,128]{2,1,0:T(8,128)(2,1)S(1)} all-to-all(bf16[16,448,128]{2,1,0:T(8,128)(2,1)S(1)} %broadcast_in_dim.16), channel_id=1, replica_groups=mesh['xh'=2,'y'=4,'core'=2,'z'=8,'xl'=2] {'xh','xl','y'}, dimensions={0} | all-to-all | bytes 3670016 | tf_op jit(solution)/shard_map/all_to_all | solution.py:389
  125.9 5.7 %collective-permute-start.3 = (bf16[7168,128]{1,0:T(8,128)(2,1)S(1)}, bf16[7168,128]{1,0:T(8,128)(2,1)}, u32[]{:S(2)}, u32[]{:S(2)}) collective-permute-start(bf16[7168,128]{1,0:T(8,128)(2,1)S(1)} %bitcast.11), channel_id=1, source_target_pairs={{0,16},{16,0},{1,17},{17,1},{2,18},{18,2},{3,19},{19,3},{4,20},{20... | collective-permute-start | bytes 5505032 | tf_op jit(solution)/shard_map/ppermute | solution.py:471
  131.7 0.8 reshape.56
  132.5 2.0 %shard_map.103 = (f32[18,256,256]{2,1,0:T(8,128)}, f32[6,256,256]{2,1,0:T(8,128)}, f32[3,256,256]{2,1,0:T(8,128)}, f32[8,256]{1,0:T(8,128)S(1)}) custom-call(s32[1]{0:T(128)} %bitcast.core_ref, bf16[7168,128]{1,0:T(8,128)(2,1)S(1)} %bitcast.12), custom_call_target="tpu_custom_call" | custom-call | bytes 6000000 | tf_op jit(solution)/shard_map/pallas_call | solution.py:422
  134.5 0.7 collective-permute-done.3.part_ref
  135.2 3.5 %shard_map.104 = (f32[18,256,256]{2,1,0:T(8,128)}, f32[6,256,256]{2,1,0:T(8,128)}, f32[3,256,256]{2,1,0:T(8,128)}, f32[8,256]{1,0:T(8,128)S(1)}) custom-call(s32[1]{0:T(128)S(6)} %sub.3.core_ref, bf16[7168,128]{1,0:T(8,128)(2,1)} %collective-permute-done.3.part_ref, ...), custom_call_target="tpu_custom_call", output_to_operand_aliasing={{0}: (2, {}), {1}: (3, {}), {2}: (4, {}), {3}: (5, {})} | custom-call | bytes 6000000 | tf_op jit(solution)/shard_map/pallas_call | solution.py:422
  138.7 0.6 slice.35
  (7 shorter events, 0.1 us)
Async XLA Ops:
  1.6 13.6 %collective-permute-start = (bf16[384,256]{1,0:T(8,128)(2,1)S(1)}, bf16[384,256]{1,0:T(8,128)(2,1)S(1)}, u32[]{:S(2)}, u32[]{:S(2)}) collective-permute-start(bf16[384,256]{1,0:T(8,128)(2,1)S(1)} %bitcast.23), channel_id=1, source_target_pairs={{0,1},{1,2},{2,3},{3,4},{4,5},{5,6},{6,7},{7,8},{8,9},{9,10},{10,1... | collective-permute-start | bytes 589832 | tf_op jit(solution)/shard_map/ppermute | solution.py:385
  7.5 7.6 %collective-permute-start.1 = (bf16[320,256]{1,0:T(8,128)(2,1)S(1)}, bf16[320,256]{1,0:T(8,128)(2,1)S(1)}, u32[]{:S(2)}, u32[]{:S(2)}) collective-permute-start(bf16[320,256]{1,0:T(8,128)(2,1)S(1)} %slice_dynamic-update-slice_fusion), channel_id=1, source_target_pairs={{1,0},{2,1},{3,2},{4,3},{5,4},{6,5},{7,6},{8,7},{9,8},{10,9},{11,1... | collective-permute-start | bytes 491528 | tf_op jit(solution)/shard_map/ppermute | solution.py:385
  8.8 1.0 copy-start
  9.8 1.7 %copy-start.2 = (bf16[2,3,3,256,256]{4,3,2,1,0:T(8,128)(2,1)S(1)}, bf16[2,3,3,256,256]{4,3,2,1,0:T(8,128)(2,1)}, u32[]{:S(2)}) copy-start(bf16[2,3,3,256,256]{4,3,2,1,0:T(8,128)(2,1)} %param.9) | copy-start | bytes 7077892
  11.5 0.7 copy-start.6
  12.2 3.0 %copy-start.1 = (bf16[1,16,8,8,256]{4,3,2,1,0:T(8,128)(2,1)S(1)}, bf16[1,16,8,8,256]{4,3,2,1,0:T(8,128)(2,1)}, u32[]{:S(2)}) copy-start(bf16[1,16,8,8,256]{4,3,2,1,0:T(8,128)(2,1)} %param.6) | copy-start | bytes 1572868
  12.2 3.0 %copy-start.3 = (bf16[2,3,3,256,256]{4,3,2,1,0:T(8,128)(2,1)S(1)}, bf16[2,3,3,256,256]{4,3,2,1,0:T(8,128)(2,1)}, u32[]{:S(2)}) copy-start(bf16[2,3,3,256,256]{4,3,2,1,0:T(8,128)(2,1)} %param.9) | copy-start | bytes 7077892
  12.2 3.0 %copy-start.4 = (bf16[2,3,256,256]{3,2,1,0:T(8,128)(2,1)S(1)}, bf16[2,3,256,256]{3,2,1,0:T(8,128)(2,1)}, u32[]{:S(2)}) copy-start(bf16[2,3,256,256]{3,2,1,0:T(8,128)(2,1)} %tw_hbm.1) | copy-start | bytes 2359300
  12.2 3.0 %copy-start.5 = (bf16[3,256,256]{2,1,0:T(8,128)(2,1)S(1)}, bf16[3,256,256]{2,1,0:T(8,128)(2,1)}, u32[]{:S(2)}) copy-start(bf16[3,256,256]{2,1,0:T(8,128)(2,1)} %rw_hbm.1) | copy-start | bytes 1179652
  12.2 3.0 %copy-start.7 = (f32[2,256]{1,0:T(2,128)S(1)}, f32[2,256]{1,0:T(2,128)}, u32[]{:S(2)}) copy-start(f32[2,256]{1,0:T(2,128)} %gains_hbm.3) | copy-start | bytes 6148
  35.8 4.7 %collective-permute-start.2 = (bf16[7168,128]{1,0:T(8,128)(2,1)S(1)}, bf16[7168,128]{1,0:T(8,128)(2,1)S(1)}, u32[]{:S(2)}, u32[]{:S(2)}) collective-permute-start(bf16[7168,128]{1,0:T(8,128)(2,1)S(1)} %get-tuple-element.24), channel_id=1, source_target_pairs={{0,16},{16,0},{1,17},{17,1},{2,18},{18,2},{3,19},{19,3},{4,20},{20... | collective-permute-start | bytes 5505032 | tf_op jit(solution)/shard_map/ppermute | solution.py:463
  125.9 9.3 %collective-permute-start.3 = (bf16[7168,128]{1,0:T(8,128)(2,1)S(1)}, bf16[7168,128]{1,0:T(8,128)(2,1)}, u32[]{:S(2)}, u32[]{:S(2)}) collective-permute-start(bf16[7168,128]{1,0:T(8,128)(2,1)S(1)} %bitcast.11), channel_id=1, source_target_pairs={{0,16},{16,0},{1,17},{17,1},{2,18},{18,2},{3,19},{19,3},{4,20},{20... | collective-permute-start | bytes 5505032 | tf_op jit(solution)/shard_map/ppermute | solution.py:471

commit v3 on v2

--- a/solution.py
+++ b/solution.py
@@ -11,15 +11,14 @@
 C = 256
 PIX = 64
 FR = 16
-UNROLL = 2
 OUT = pltpu.VMEM
 HBM = pltpu.HBM
 MATS = 27
 ROWS = MATS * C
 CHUNK = 448
 FLAT = 16 * CHUNK
-EVERY = ("xh", "y", "core", "z", "xl")
-PLANE = ("xh", "xl", "y")
+EVERY = ("xh", "y", "core", "zh", "zl", "xl")
+PLANE = ("xh", "xl", "y", "zl")
 
 
 def dot(left, right):
@@ -93,7 +92,7 @@
             n_ref[rows, :] = value.astype(BF16)
         return 0
 
-    lax.fori_loop(0, count, body, 0, unroll=UNROLL)
+    lax.fori_loop(0, count, body, 0, unroll=True)
 
 
 def activate(im, weights, pieces, act, slope):
@@ -265,7 +264,7 @@
             write_windows(ga[rows, :] * slope[one_frame(index + slope_own), :], im, rows, -1)
             return 0
 
-        lax.fori_loop(0, count, body, 0, unroll=UNROLL)
+        lax.fori_loop(0, count, body, 0, unroll=True)
         for tap in range(9):
             wcat[:, tap * C : (tap + 1) * C] = sw_ref[block, tap]
         for first, size in pieces:
@@ -294,8 +293,8 @@
         return total + jnp.sum((grad * unit).reshape(8, 8, C), axis=0)
 
     none = jnp.zeros((8, C), F32)
-    total2 = lax.fori_loop(0, FR, norm_back, none, unroll=UNROLL)
-    lax.fori_loop(FR, FR + 2, norm_back, none)
+    total2 = lax.fori_loop(0, FR, norm_back, none, unroll=True)
+    lax.fori_loop(FR, FR + 2, norm_back, none, unroll=True)
 
     block_back(0, g1, a1, 6, slope1, 0, 16, [(0, 512), (512, 512)])
 
@@ -303,7 +302,7 @@
         grad, unit, _ = gain_part(index, s1, 6)
         return total + jnp.sum((grad * unit).reshape(8, 8, C), axis=0)
 
-    total1 = lax.fori_loop(0, FR, gain_only, none, unroll=UNROLL)
+    total1 = lax.fori_loop(0, FR, gain_only, none, unroll=True)
     rest = jnp.concatenate(
         [
             jnp.sum(total1, axis=0, keepdims=True),
@@ -323,6 +322,9 @@
 
     whole = pl.BlockSpec(memory_space=pltpu.VMEM)
     hbm = pl.BlockSpec(memory_space=HBM)
+    video, gains, sw, tw, rw = (
+        pltpu.with_memory_space_constraint(value, HBM) for value in (video, gains, sw, tw, rw)
+    )
     normed, act, slope = pl.pallas_call(
         front_kernel,
         out_shape=(OUT((FR * PIX, C), BF16), OUT((FR * PIX, C), BF16), OUT((FR * PIX, C), F32)),
@@ -396,7 +398,7 @@
 
 
 def place_kernel(core_ref, part_ref, *refs):
-    sp_ref, tm_ref, dn_ref, gn_ref, buf, gains, sems = refs[-7:]
+    sp_ref, tm_ref, dn_ref, buf, sems = refs[-5:]
     lanes = pl.ds(pl.multiple_of(core_ref[0] * 128, 128), 128)
     copies = []
     for matrix in range(MATS):
@@ -409,9 +411,6 @@
             target = dn_ref.at[matrix - 24, :, lanes]
         copies.append(pltpu.make_async_copy(buf.at[matrix], target, sems.at[matrix]))
         copies[-1].start()
-    gains[...] = part_ref[ROWS : ROWS + 16, :].astype(F32)[:8]
-    copies.append(pltpu.make_async_copy(gains, gn_ref.at[:, lanes], sems.at[MATS]))
-    copies[-1].start()
     for copy in copies:
         copy.wait()
 
@@ -425,15 +424,10 @@
             jax.ShapeDtypeStruct((18, C, C), F32),
             jax.ShapeDtypeStruct((6, C, C), F32),
             jax.ShapeDtypeStruct((3, C, C), F32),
-            jax.ShapeDtypeStruct((8, C), F32),
         ),
         in_specs=[pl.BlockSpec(memory_space=pltpu.SMEM), whole] + [hbm] * len(outputs),
-        out_specs=(hbm,) * 4,
-        scratch_shapes=[
-            pltpu.VMEM((MATS, C, 128), F32),
-            pltpu.VMEM((8, 128), F32),
-            pltpu.SemaphoreType.DMA((MATS + 1,)),
-        ],
+        out_specs=(hbm,) * 3,
+        scratch_shapes=[pltpu.VMEM((MATS, C, 128), F32), pltpu.SemaphoreType.DMA((MATS,))],
         input_output_aliases={2 + i: i for i in range(len(outputs))},
         compiler_params=pltpu.CompilerParams(vmem_limit_bytes=16 * 1024 * 1024),
         cost_estimate=pl.CostEstimate(flops=0, bytes_accessed=6_000_000, transcendentals=0),
@@ -441,7 +435,7 @@
 
 
 def on_device(video, cotangent, gains, spatial_weights, time_weights, reduce_kernel_weights):
-    tm = ("z", "xl")
+    tm = ("zh", "zl", "xl")
     video = video.reshape(FR * PIX, C)
     cot = cotangent.reshape(FR * 8, 4 * C)
     before = passed_along(video[-6 * PIX :], tm, 1)
@@ -462,27 +456,30 @@
     swap = [(0, 1), (1, 0)]
     other = lax.ppermute(theirs, "core", swap)
     half = (mine.astype(F32) + other.astype(F32)).astype(BF16)
-    parts = exchange(half, PLANE).reshape(16, CHUNK, 128)
+    parts = exchange(half, PLANE).reshape(32, FLAT // 32, 128)
     part = jnp.sum(parts.astype(F32), axis=0).astype(BF16)
-    parts = exchange(part, "z").reshape(8, CHUNK // 8, 128)
+    parts = to_all(part, "zh", 4).reshape(4, FLAT // 32, 128)
     part = jnp.sum(parts.astype(F32), axis=0).astype(BF16)
-    part = to_all(part, "z", 8)
-    mine = to_all(part, PLANE, 16)
+    mine = to_all(part, PLANE, 32)
     other = lax.ppermute(mine, "core", swap)
     outputs = place(core, mine)
-    grad_sp, grad_tm, grad_dn, grad_gn = place(1 - core, other, outputs)
+    grad_sp, grad_tm, grad_dn = place(1 - core, other, outputs)
+    own_gn, other_gn = mine[ROWS : ROWS + 2].astype(F32), other[ROWS : ROWS + 2].astype(F32)
+    grad_gn = jnp.concatenate(
+        [jnp.where(core == 0, own_gn, other_gn), jnp.where(core == 0, other_gn, own_gn)], axis=1
+    )
     return (
         encoded.reshape(1, FR // 2, 4, 4, 4 * C),
         grad_sp.reshape(2, 3, 3, C, C),
         grad_tm.reshape(2, 3, C, C),
         grad_dn,
-        grad_gn[:2],
+        grad_gn,
     )
 
 
 def solution(mesh):
-    fine = Mesh(mesh.devices.reshape(2, 4, 2, 8, 2), EVERY)
-    split = P(("xh", "y", "core"), ("z", "xl"), None, None, None)
+    fine = Mesh(mesh.devices.reshape(2, 4, 2, 4, 2, 2), EVERY)
+    split = P(("xh", "y", "core"), ("zh", "zl", "xl"), None, None, None)
     return jax.shard_map(
         on_device,
         mesh=fine,

time: 140 us -> 125 us (0.89)
  blocking collectives: 84.3 us -> 76 us
  Pallas kernels: 29.1 us -> 23.6 us
  local copies, waits for them, and re-layouts: 7.98 us -> 3.91 us
  waiting for transfers between devices: 4.12 us -> 6.72 us
    all_to_all x4 -> x3, blocking collectives: 84.3 us -> 76 us  [exchange(): return lax.all_to_all(value, axes, split_axis=0, concat_axis=0, tiled=True)]
    pallas_call x1, Pallas kernels: 20.7 us -> 15.1 us  [run_model(): pl.pallas_call(model_kernel, out_shape=(jax.ShapeDtypeStruct((128, 4 * C)...]
    unnamed x20 -> x4, local copies, waits for them, and re-layouts: 3.43 us -> 0.02 us
    ppermute x2, waiting for transfers between devices: 0.01 us -> 2.59 us  [passed_along(): lax.ppermute(value, axes, [(source, source + steps) for source in range(f...]
  transfers between devices with their start and end apart: 4 -> 4, of which waited for: 2 -> 3; matrix products, arithmetic and copies ran while one was open for 2% -> 2% of each run, Pallas kernels for 4% -> 4%
where the time goes in v3:
time: 125 us
  blocking collectives  76 us (61%)
  Pallas kernels  23.6 us (19%)
  starting transfers between devices  11.5 us (9%)
  waiting for transfers between devices  6.72 us (5%)
  local copies, waits for them, and re-layouts  3.91 us (3%)
  other arithmetic  2.04 us (2%)
    all_to_all x3, blocking collectives, exchange(): return lax.all_to_all(value, axes, split_axis=0, concat_axis=0, tiled=True)  76 us
    pallas_call x1, Pallas kernels, run_model(): pl.pallas_call(model_kernel, out_shape=(jax.ShapeDtypeStruct((128, 4 * C)...  15.1 us
    pallas_call x2, Pallas kernels, place(): pl.pallas_call(place_kernel, out_shape=(jax.ShapeDtypeStruct((18, C, C),...  5.52 us
    ppermute x2, starting transfers between devices, passed_along(): lax.ppermute(value, axes, [(source, source + steps) for source in range(f...  5.25 us
    ppermute x1, starting transfers between devices, on_device(): other = lax.ppermute(mine, 'core', swap)  4.45 us
    ppermute x1, waiting for transfers between devices, on_device(): other = lax.ppermute(theirs, 'core', swap)  3.41 us
    pallas_call x1, Pallas kernels, run_model(): pl.pallas_call(front_kernel, out_shape=(OUT((FR * PIX, C), BF16), OUT((FR...  3.05 us
    ppermute x2, waiting for transfers between devices, passed_along(): lax.ppermute(value, axes, [(source, source + steps) for source in range(f...  2.59 us
  transfers between devices with their start and end apart: 4, of which 3 were waited for; matrix products, arithmetic and copies ran while one was open for 2% of the time, Pallas kernels for 4%

profile of v3, /device:TPU:1, one launch (start us, length us, event | category | flops | bytes accessed | tf_op | source)
XLA Modules:
  0.0 124.7 jit_solution(12950545946803249551)
XLA Ops:
  0.6 0.9 slice.30
  1.6 4.0 %collective-permute-start = (bf16[384,256]{1,0:T(8,128)(2,1)S(1)}, bf16[384,256]{1,0:T(8,128)(2,1)S(1)}, u32[]{:S(2)}, u32[]{:S(2)}) collective-permute-start(bf16[384,256]{1,0:T(8,128)(2,1)S(1)} %bitcast.17), channel_id=1, source_target_pairs={{0,1},{1,2},{2,3},{3,4},{4,5},{5,6},{6,7},{7,8},{8,9},{9,10},{10,1... | collective-permute-start | bytes 589832 | tf_op jit(solution)/shard_map/ppermute | solution.py:387
  5.5 0.8 slice.32
  6.4 1.0 reshape.53.cot_ref
  7.5 1.3 %collective-permute-start.1 = (bf16[320,256]{1,0:T(8,128)(2,1)S(1)}, bf16[320,256]{1,0:T(8,128)(2,1)S(1)}, u32[]{:S(2)}, u32[]{:S(2)}) collective-permute-start(bf16[320,256]{1,0:T(8,128)(2,1)S(1)} %slice_dynamic-update-slice_fusion), channel_id=1, source_target_pairs={{1,0},{2,1},{3,2},{4,3},{5,4},{6,5},{7,6},{8,7},{9,8},{10,9},{11,1... | collective-permute-start | bytes 491528 | tf_op jit(solution)/shard_map/ppermute | solution.py:387
  8.8 3.1 %shard_map.101 = (bf16[1024,256]{1,0:T(8,128)(2,1)S(1)}, bf16[1024,256]{1,0:T(8,128)(2,1)S(1)}, f32[1024,256]{1,0:T(8,128)S(1)}) custom-call(bf16[1024,256]{1,0:T(8,128)(2,1)} %bitcast.18, f32[2,256]{1,0:T(2,128)} %gains_hbm.3, bf16[2,9,256,256]{3,2,1,0:T(8,128)(2,1)} %bitcast.20), custom_call_target="tpu_custom_call" | custom-call | flops 1200000000 | bytes 4000000 | tf_op jit(solution)/shard_map/pallas_call | solution.py:328
  11.8 2.6 %collective-permute-done.1.after_ref = bf16[320,256]{1,0:T(8,128)(2,1)S(1)} collective-permute-done((bf16[320,256]{1,0:T(8,128)(2,1)S(1)}, bf16[320,256]{1,0:T(8,128)(2,1)S(1)}, u32[]{:S(2)}, u32[]{:S(2)}) %collective-permute-start.1) | collective-permute-done | bytes 163872 | tf_op jit(solution)/shard_map/ppermute | solution.py:387
  14.4 0.0 collective-permute-done.before_ref
  14.4 15.1 %shard_map.102 = (bf16[128,1024]{1,0:T(8,128)(2,1)S(1)}, bf16[7168,128]{1,0:T(8,128)(2,1)S(1)}, bf16[7168,128]{1,0:T(8,128)(2,1)S(1)}) custom-call(s32[1]{0:T(128)} %bitcast.core_ref, bf16[1024,256]{1,0:T(8,128)(2,1)S(1)} %get-tuple-element.17.n1_ref, bf16[1024,256]{1,0:T(8,128)(2,1)S(1)} %get-tuple-element.18.a1_ref, ...), custom_call_target="tpu_custom_call" | custom-call | flops 10000000000 | bytes 8000000 | tf_op jit(solution)/shard_map/pallas_call | solution.py:345
  29.5 1.8 %collective-permute-start.2 = (bf16[7168,128]{1,0:T(8,128)(2,1)S(1)}, bf16[7168,128]{1,0:T(8,128)(2,1)S(1)}, u32[]{:S(2)}, u32[]{:S(2)}) collective-permute-start(bf16[7168,128]{1,0:T(8,128)(2,1)S(1)} %get-tuple-element.22), channel_id=1, source_target_pairs={{0,16},{16,0},{1,17},{17,1},{2,18},{18,2},{3,19},{19,3},{4,20},{20... | collective-permute-start | bytes 5505032 | tf_op jit(solution)/shard_map/ppermute | solution.py:457
  31.3 3.4 %collective-permute-done.2 = bf16[7168,128]{1,0:T(8,128)(2,1)S(1)} collective-permute-done((bf16[7168,128]{1,0:T(8,128)(2,1)S(1)}, bf16[7168,128]{1,0:T(8,128)(2,1)S(1)}, u32[]{:S(2)}, u32[]{:S(2)}) %collective-permute-start.2) | collective-permute-done | bytes 1835040 | tf_op jit(solution)/shard_map/ppermute | solution.py:457
  34.7 0.5 add_convert_fusion
  35.2 34.8 %all_to_all.23 = bf16[32,224,128]{2,1,0:T(8,128)(2,1)S(1)} all-to-all(bf16[32,224,128]{2,1,0:T(8,128)(2,1)S(1)} %bitcast.13), channel_id=1, replica_groups=mesh['xh'=2,'y'=4,'core'=2,'zh'=4,'zl'=2,'xl'=2] {'xh','xl','y','zl'}, dimensions={0} | all-to-all | bytes 3670016 | tf_op jit(solution)/shard_map/all_to_all | solution.py:391
  70.0 0.3 reduce_sum.24
  70.3 14.5 %all_to_all.24 = bf16[4,224,128]{2,1,0:T(8,128)(2,1)S(1)} all-to-all(bf16[4,224,128]{2,1,0:T(8,128)(2,1)S(1)} %broadcast_in_dim.23), channel_id=1, replica_groups=mesh['xh'=2,'y'=4,'core'=2,'zh'=4,'zl'=2,'xl'=2] {'zh'}, dimensions={0} | all-to-all | bytes 458752 | tf_op jit(solution)/shard_map/all_to_all | solution.py:391
  84.8 0.2 broadcast_in_dim.24
  85.1 26.6 %all_to_all.25 = bf16[32,224,128]{2,1,0:T(8,128)(2,1)S(1)} all-to-all(bf16[32,224,128]{2,1,0:T(8,128)(2,1)S(1)} %broadcast_in_dim.24), channel_id=1, replica_groups=mesh['xh'=2,'y'=4,'core'=2,'zh'=4,'zl'=2,'xl'=2] {'xh','xl','y','zl'}, dimensions={0} | all-to-all | bytes 3670016 | tf_op jit(solution)/shard_map/all_to_all | solution.py:391
  111.7 4.5 %collective-permute-start.3 = (bf16[7168,128]{1,0:T(8,128)(2,1)S(1)}, bf16[7168,128]{1,0:T(8,128)(2,1)}, u32[]{:S(2)}, u32[]{:S(2)}) collective-permute-start(bf16[7168,128]{1,0:T(8,128)(2,1)S(1)} %bitcast.10), channel_id=1, source_target_pairs={{0,16},{16,0},{1,17},{17,1},{2,18},{18,2},{3,19},{19,3},{4,20},{20... | collective-permute-start | bytes 5505032 | tf_op jit(solution)/shard_map/ppermute | solution.py:464
  116.2 0.8 reshape.54
  117.0 2.0 %shard_map.103 = (f32[18,256,256]{2,1,0:T(8,128)}, f32[6,256,256]{2,1,0:T(8,128)}, f32[3,256,256]{2,1,0:T(8,128)}) custom-call(s32[1]{0:T(128)} %bitcast.core_ref, bf16[7168,128]{1,0:T(8,128)(2,1)S(1)} %bitcast.11), custom_call_target="tpu_custom_call" | custom-call | bytes 6000000 | tf_op jit(solution)/shard_map/pallas_call | solution.py:421
  119.0 0.7 collective-permute-done.3.part_ref
  119.7 0.7 convert_select_fusion.1
  120.4 0.6 pad_maximum_fusion
  121.0 3.5 %shard_map.104 = (f32[18,256,256]{2,1,0:T(8,128)}, f32[6,256,256]{2,1,0:T(8,128)}, f32[3,256,256]{2,1,0:T(8,128)}) custom-call(s32[1]{0:T(128)S(6)} %sub.3.core_ref, bf16[7168,128]{1,0:T(8,128)(2,1)} %collective-permute-done.3.part_ref, f32[18,256,256]{2,1,0:T(8,128)} %get-tuple-element.23.refs_0_, ...), custom_call_target="tpu_custom_call", output_to_operand_aliasing={{0}: (2, {}), {1}: (3, {}), {2}: (4, {})} | custom-call | bytes 6000000 | tf_op jit(solution)/shard_map/pallas_call | solution.py:421
  (7 shorter events, 0.1 us)
Async XLA Ops:
  1.6 12.9 %collective-permute-start = (bf16[384,256]{1,0:T(8,128)(2,1)S(1)}, bf16[384,256]{1,0:T(8,128)(2,1)S(1)}, u32[]{:S(2)}, u32[]{:S(2)}) collective-permute-start(bf16[384,256]{1,0:T(8,128)(2,1)S(1)} %bitcast.17), channel_id=1, source_target_pairs={{0,1},{1,2},{2,3},{3,4},{4,5},{5,6},{6,7},{7,8},{8,9},{9,10},{10,1... | collective-permute-start | bytes 589832 | tf_op jit(solution)/shard_map/ppermute | solution.py:387
  7.5 7.0 %collective-permute-start.1 = (bf16[320,256]{1,0:T(8,128)(2,1)S(1)}, bf16[320,256]{1,0:T(8,128)(2,1)S(1)}, u32[]{:S(2)}, u32[]{:S(2)}) collective-permute-start(bf16[320,256]{1,0:T(8,128)(2,1)S(1)} %slice_dynamic-update-slice_fusion), channel_id=1, source_target_pairs={{1,0},{2,1},{3,2},{4,3},{5,4},{6,5},{7,6},{8,7},{9,8},{10,9},{11,1... | collective-permute-start | bytes 491528 | tf_op jit(solution)/shard_map/ppermute | solution.py:387
  29.5 5.2 %collective-permute-start.2 = (bf16[7168,128]{1,0:T(8,128)(2,1)S(1)}, bf16[7168,128]{1,0:T(8,128)(2,1)S(1)}, u32[]{:S(2)}, u32[]{:S(2)}) collective-permute-start(bf16[7168,128]{1,0:T(8,128)(2,1)S(1)} %get-tuple-element.22), channel_id=1, source_target_pairs={{0,16},{16,0},{1,17},{17,1},{2,18},{18,2},{3,19},{19,3},{4,20},{20... | collective-permute-start | bytes 5505032 | tf_op jit(solution)/shard_map/ppermute | solution.py:457
  111.7 8.0 %collective-permute-start.3 = (bf16[7168,128]{1,0:T(8,128)(2,1)S(1)}, bf16[7168,128]{1,0:T(8,128)(2,1)}, u32[]{:S(2)}, u32[]{:S(2)}) collective-permute-start(bf16[7168,128]{1,0:T(8,128)(2,1)S(1)} %bitcast.10), channel_id=1, source_target_pairs={{0,16},{16,0},{1,17},{17,1},{2,18},{18,2},{3,19},{19,3},{4,20},{20... | collective-permute-start | bytes 5505032 | tf_op jit(solution)/shard_map/ppermute | solution.py:464

commit v4 on v2

v4 whole, which is shorter than its diff:
```python
import jax
import jax.numpy as jnp
from jax import lax
from jax.experimental import pallas as pl
from jax.experimental.pallas import tpu as pltpu
from jax.sharding import Mesh, PartitionSpec as P

EPSILON = 1e-06
F32 = jnp.float32
BF16 = jnp.bfloat16
C = 256
PIX = 64
FR = 16
OUT = pltpu.VMEM
HBM = pltpu.HBM
MATS = 27
ROWS = MATS * C
CHUNK = 448
FLAT = 16 * CHUNK
EVERY = ("xh", "y", "core", "z", "xl")


def dot(left, right):
    return jnp.dot(left, right, preferred_element_type=F32)


def dot_nt(left, right):
    return lax.dot_general(left, right, (((1,), (1,)), ((), ())), preferred_element_type=F32)


def dot_tn(left, right):
    return lax.dot_general(left, right, (((0,), (0,)), ((), ())), preferred_element_type=F32)


def frames(first, count):
    return pl.ds(first * PIX, count * PIX)


def one_frame(index):
    return pl.ds(pl.multiple_of(index * PIX, PIX), PIX)


def write_windows(value, im_ref, rows, sign):
    grid = value.reshape(8, 8, C)
    column = lax.broadcasted_iota(jnp.int32, (8, 8, C), 1)
    blank = jnp.zeros((1, 8, C), F32)
    for j in range(3):
        dx = sign * (j - 1)
        if dx == 0:
            moved = grid
        elif dx == 1:
            moved = jnp.where(column == 7, 0.0, pltpu.roll(grid, 7, 1))
        else:
            moved = jnp.where(column == 0, 0.0, pltpu.roll(grid, 1, 1))
        for i in range(3):
            dy = sign * (i - 1)
            if dy == 0:
                placed = moved
            elif dy == 1:
                placed = jnp.concatenate([moved[1:], blank], axis=0)
            else:
                placed = jnp.concatenate([blank, moved[:-1]], axis=0)
            tap = 3 * i + j
            im_ref[rows, tap * C : (tap + 1) * C] = placed.reshape(PIX, C).astype(BF16)


def place_matrix(groups):
    size = groups * 8
    dest = lax.broadcasted_iota(jnp.int32, (size, size), 0)
    src = lax.broadcasted_iota(jnp.int32, (size, size), 1)
    want = (dest & 1) * (groups * 4) + (dest >> 3) * 4 + ((dest >> 1) & 3)
    return jnp.where(src == want, 1.0, 0.0).astype(BF16)


def ungroup(piece, groups, one_hot):
    halves = []
    for i in range(2):
        both = jnp.concatenate([piece(2 * i + j) for j in range(2)], axis=0)
        halves.append(dot(one_hot, both).reshape(groups, 8, C))
    return jnp.concatenate(halves, axis=1).reshape(groups * 16, C).astype(BF16)


def norm_only(src, first, count, gain, n_ref, to):
    for index in range(count):
        value = src[frames(first + index, 1), :].astype(F32)
        inv = lax.rsqrt(jnp.mean(value * value, axis=-1, keepdims=True) + EPSILON)
        n_ref[frames(to + index, 1), :] = (value * inv * gain).astype(BF16)


def norm_windows(src, first, count, gain, im, n_ref=None):
    def body(index, _):
        rows = one_frame(index)
        value = src[one_frame(index + first), :].astype(F32)
        inv = lax.rsqrt(jnp.mean(value * value, axis=-1, keepdims=True) + EPSILON)
        value = value * inv * gain
        write_windows(value, im, rows, 1)
        if n_ref is not None:
            n_ref[rows, :] = value.astype(BF16)
        return 0

    lax.fori_loop(0, count, body, 0, unroll=True)


def activate(im, weights, pieces, act, slope):
    for first, size, act_first, slope_first in pieces:
        conv = dot(im[pl.ds(first, size), :], weights.reshape(9 * C, C))
        logistic = jax.nn.sigmoid(conv)
        act[pl.ds(act_first, size), :] = (conv * logistic).astype(BF16)
        if slope_first is not None:
            slope_value = logistic * (1.0 + conv * (1.0 - logistic))
            slope[pl.ds(slope_first, size), :] = slope_value.astype(slope.dtype)


def side_by_side(raw_ref, count, flat_ref):
    for group in range(count):
        rows = raw_ref[group].astype(F32)
        for tap in range(4):
            first = tap * count * 4 + group * 4
            flat_ref[first : first + 4, :] = rows[:, tap * C : (tap + 1) * C]


def edge_kernel(video_hbm, cot_hbm, last_ref, first_ref, raw, flat, sems):
    copies = [
        pltpu.make_async_copy(cot_hbm.at[pl.ds(0, 12)], raw, sems.at[0]),
        pltpu.make_async_copy(video_hbm.at[frames(10, 6)], last_ref, sems.at[1]),
        pltpu.make_async_copy(video_hbm.at[frames(0, 2)], first_ref.at[frames(0, 2)], sems.at[2]),
    ]
    for copy in copies:
        copy.start()
    copies[0].wait()
    side_by_side(raw, 12, flat)
    first_ref[2 * PIX :, :] = flat[...].astype(BF16)
    copies[1].wait()
    copies[2].wait()


def edges(video, cot):
    whole = pl.BlockSpec(memory_space=pltpu.VMEM)
    hbm = pl.BlockSpec(memory_space=HBM)
    return pl.pallas_call(
        edge_kernel,
        out_shape=(OUT((6 * PIX, C), BF16), OUT((5 * PIX, C), BF16)),
        in_specs=[hbm, hbm],
        out_specs=(whole, whole),
        scratch_shapes=[
            pltpu.VMEM((12, 4, 4 * C), BF16),
            pltpu.VMEM((3 * PIX, C), F32),
            pltpu.SemaphoreType.DMA((3,)),
        ],
        compiler_params=pltpu.CompilerParams(vmem_limit_bytes=8 * 1024 * 1024),
        cost_estimate=pl.CostEstimate(flops=0, bytes_accessed=1_000_000, transcendentals=0),
    )(video, cot)


def with_edge(act, first, count):
    return jnp.concatenate([act[frames(first - k, count), :] for k in range(3)], axis=1)


def unpacked(pack_ref):
    return [pack_ref.at[frames(first, count)] for first, count in ((0, 16), (16, 14), (30, 14))]


def front_kernel(
    video_hbm,
    gains_hbm,
    sw_hbm,
    tw_hbm,
    pack_ref,
    slope1_ref,
    s2_ref,
    gains,
    sw_ref,
    tw_ref,
    im1,
    im2,
    video,
    sems,
):
    a1_ref, a2_ref, slope2_ref = unpacked(pack_ref)
    pairs = [
        (video_hbm, video),
        (gains_hbm, gains),
        (sw_hbm.at[0], sw_ref.at[0]),
        (tw_hbm, tw_ref),
        (sw_hbm.at[1], sw_ref.at[1]),
    ]
    copies = [pltpu.make_async_copy(*pair, sems.at[i]) for i, pair in enumerate(pairs)]
    for copy in copies:
        copy.start()
    copies[0].wait()
    copies[1].wait()
    norm_windows(video, 0, FR, gains[0:1, :], im1)
    for copy in copies[2:]:
        copy.wait()
    activate(im1, sw_ref[0], [(0, 512, 0, 0), (512, 512, 512, 512)], a1_ref, slope1_ref)
    later = with_edge(a1_ref, 2, 14)
    s2_ref[...] = video[frames(2, 14), :].astype(F32) + dot(later, tw_ref[0].reshape(3 * C, C))
    norm_windows(s2_ref, 0, 14, gains[1:2, :], im2)
    activate(im2, sw_ref[1], [(0, 448, 0, 0), (448, 448, 448, 448)], a2_ref, slope2_ref)


def model_kernel(
    core_ref,
    before_ref,
    after_ref,
    gains_hbm,
    sw_hbm,
    tw_hbm,
    rw_hbm,
    video_hbm,
    cot_hbm,
    pack_ref,
    slope1,
    s2_own,
    enc_ref,
    mine_ref,
    theirs_ref,
    s1,
    s2,
    im,
    n2_ref,
    a1,
    a2,
    slope2,
    low,
    cotf,
    up,
    g2,
    g1,
    ga,
    gn,
    wcat,
    gains_ref,
    sw_ref,
    tw_ref,
    rw_ref,
    s1_own,
    n1_ref,
    cot_raw,
    cot_flat,
    sems,
):
    pairs = [
        (gains_hbm, gains_ref),
        (sw_hbm.at[0], sw_ref.at[0]),
        (tw_hbm, tw_ref),
        (video_hbm, s1_own),
        (sw_hbm.at[1], sw_ref.at[1]),
        (rw_hbm, rw_ref),
        (cot_hbm, cot_raw),
    ]
    copies = [pltpu.make_async_copy(*pair, sems.at[i]) for i, pair in enumerate(pairs)]
    for copy in copies:
        copy.start()
    s1[frames(0, 6), :] = before_ref[...].astype(F32)
    s1[frames(22, 2), :] = after_ref[: 2 * PIX].astype(F32)
    a1_own, a2_own, slope2_own = unpacked(pack_ref)
    a1[frames(6, 16), :] = a1_own[...]
    s2[frames(5, 14), :] = s2_own[...]
    a2[frames(5, 14), :] = a2_own[...]
    slope2[frames(5, 14), :] = slope2_own[...].astype(F32)
    n_refs = (n1_ref, n2_ref)
    first_core = core_ref[0] == 0

    def put_halves(rows, value):
        low_half = value[:, :128].astype(BF16)
        high_half = value[:, 128:].astype(BF16)
        mine_ref[rows, :] = jnp.where(first_core, low_half, high_half)
        theirs_ref[rows, :] = jnp.where(first_core, high_half, low_half)

    def put(matrix, value):
        put_halves(pl.ds(matrix * C, C), value)

    copies[0].wait()
    norm_windows(s1, 0, 6, gains_ref[0:1, :], im)
    norm_windows(s1, 22, 2, gains_ref[0:1, :], im.at[frames(6, 2)])
    for copy in copies[1:]:
        copy.wait()
    activate(im, sw_ref[0], [(0, 384, 0, None), (384, 128, 1408, None)], a1, None)
    norm_only(s1_own, 0, FR, gains_ref[0:1, :], n1_ref, 0)
    norm_only(s2, 5, 14, gains_ref[1:2, :], n2_ref, 2)
    side_by_side(cot_raw, 32, cot_flat)
    ends = jnp.concatenate([with_edge(a1, 3, 5), with_edge(a1, 22, 2)], axis=0)
    ends = dot(ends, tw_ref[0].reshape(3 * C, C))
    s2[frames(0, 3), :] = s1[frames(3, 3), :] + ends[: 3 * PIX]
    s2[frames(3, 2), :] = s1_own[frames(0, 2), :].astype(F32) + ends[3 * PIX : 5 * PIX]
    s2[frames(19, 2), :] = s1[frames(22, 2), :] + ends[5 * PIX :]
    norm_windows(s2, 0, 3, gains_ref[1:2, :], im.at[frames(8, 3)])
    norm_windows(s2, 3, 2, gains_ref[1:2, :], im.at[frames(11, 2)], n2_ref)
    norm_windows(s2, 19, 2, gains_ref[1:2, :], im.at[frames(13, 2)])
    activate(im, sw_ref[1], [(512, 320, 0, 0), (832, 128, 1216, 1216)], a2, slope2)
    total = dot(with_edge(a2, 2, 17), tw_ref[1].reshape(3 * C, C))
    low[frames(0, 17), :] = (s2[frames(2, 17), :] + total).astype(BF16)
    low[frames(17, 1), :] = jnp.zeros((PIX, C), BF16)

    pairs = low[...].reshape(9, 2 * PIX, C)
    taps = jnp.concatenate(
        [
            pairs[1:9, :PIX].reshape(8 * PIX, C),
            pairs[0:8, PIX:].reshape(8 * PIX, C),
            pairs[0:8, :PIX].reshape(8 * PIX, C),
        ],
        axis=1,
    )
    one_hot = place_matrix(32)
    down = dot(taps, rw_ref[...].reshape(3 * C, C)).astype(BF16).astype(F32)
    down = down.reshape(32, 16, C)
    for i in range(2):
        both = dot_tn(one_hot, down[:, i * 8 : (i + 1) * 8].reshape(256, C).astype(BF16))
        for j in range(2):
            tap = 2 * i + j
            enc_ref[:, tap * C : (tap + 1) * C] = both[j * 128 : (j + 1) * 128].astype(BF16)
    cotf[frames(0, 8), :] = ungroup(
        lambda tap: cot_flat[tap * 128 : (tap + 1) * 128, :].astype(BF16), 32, one_hot
    )
    cotf[frames(8, 3), :] = ungroup(
        lambda tap: after_ref[2 * PIX + tap * 48 : 2 * PIX + (tap + 1) * 48, :],
        12,
        place_matrix(12),
    )
    grad_down = dot_tn(taps, cotf[frames(0, 8), :])
    for k in range(3):
        put(24 + k, grad_down[k * C : (k + 1) * C])
    even = dot_nt(cotf[frames(0, 10), :], rw_ref[1])
    odd = dot_nt(cotf[frames(0, 10), :], rw_ref[0]) + dot_nt(cotf[frames(1, 10), :], rw_ref[2])
    merged = jnp.concatenate(
        [even.reshape(10, PIX, C), odd.reshape(10, PIX, C)], axis=1
    ).reshape(20 * PIX, C)
    up[...] = merged[: 18 * PIX]
    g2[...] = merged.astype(BF16)

    def block_back(block, grad, act, own, slope, slope_own, count, pieces):
        grad_time = dot_tn(with_edge(act, own, FR), grad[frames(0, FR), :])
        for k in range(3):
            put(18 + 3 * block + k, grad_time[k * C : (k + 1) * C])
        for k in range(3):
            wcat[:, k * C : (k + 1) * C] = tw_ref[block, k]
        for first, size in pieces:
            later = jnp.concatenate(
                [grad[pl.ds(first + k * PIX, size), :] for k in range(3)], axis=1
            )
            ga[pl.ds(first, size), :] = dot_nt(later, wcat[:, : 3 * C])

        def body(index, _):
            rows = one_frame(index)
            write_windows(ga[rows, :] * slope[one_frame(index + slope_own), :].astype(F32), im, rows, -1)
            return 0

        lax.fori_loop(0, count, body, 0, unroll=True)
        for tap in range(9):
            wcat[:, tap * C : (tap + 1) * C] = sw_ref[block, tap]
        for first, size in pieces:
            gn[pl.ds(first, size), :] = dot_nt(im[pl.ds(first, size), :], wcat[...])
        grad_sp = dot_tn(n_refs[block][...], im[frames(0, FR), :])
        for tap in range(9):
            put(9 * block + tap, grad_sp[:, tap * C : (tap + 1) * C])

    def gain_part(index, src, own):
        value = src[one_frame(index + own), :].astype(F32)
        inv = lax.rsqrt(jnp.mean(value * value, axis=-1, keepdims=True) + EPSILON)
        unit = value * inv
        grad = gn[one_frame(index), :]
        return grad, unit, inv

    block_back(1, g2, a2, 3, slope2, 3, 18, [(0, 576), (576, 576)])
    gain = gains_ref[1:2, :]

    def norm_back(index, total):
        grad, unit, inv = gain_part(index, s2, 3)
        scaled = grad * gain
        back = inv * (scaled - unit * jnp.mean(unit * scaled, axis=-1, keepdims=True))
        rows = one_frame(index)
        g1[rows, :] = (up[rows, :] + back).astype(BF16)
        return total + jnp.sum((grad * unit).reshape(8, 8, C), axis=0)

    none = jnp.zeros((8, C), F32)
    total2 = lax.fori_loop(0, FR, norm_back, none, unroll=True)
    lax.fori_loop(FR, FR + 2, norm_back, none, unroll=True)

    block_back(0, g1, a1, 6, slope1, 0, 16, [(0, 512), (512, 512)])

    def gain_only(index, total):
        grad, unit, _ = gain_part(index, s1_own, 0)
        return total + jnp.sum((grad * unit).reshape(8, 8, C), axis=0)

    total1 = lax.fori_loop(0, FR, gain_only, none, unroll=True)
    rest = jnp.concatenate(
        [
            jnp.sum(total1, axis=0, keepdims=True),
            jnp.sum(total2, axis=0, keepdims=True),
            jnp.zeros((14, C), F32),
        ],
        axis=0,
    )
    put_halves(pl.ds(ROWS, 16), rest)
    for ref in (mine_ref, theirs_ref):
        ref[ROWS + 16 :, :] = jnp.zeros((FLAT - ROWS - 16, 128), BF16)


def run_model(core, video, before, after, cot, gains, sw, tw, rw):
    def vm(rows, dtype, cols=C):
        return pltpu.VMEM((rows * PIX, cols), dtype)

    whole = pl.BlockSpec(memory_space=pltpu.VMEM)
    hbm = pl.BlockSpec(memory_space=HBM)
    own = [(44, BF16), (16, F32), (14, F32)]
    known = pl.pallas_call(
        front_kernel,
        out_shape=tuple(OUT((count * PIX, C), dtype) for count, dtype in own),
        in_specs=[hbm] * 4,
        out_specs=(whole,) * 3,
        scratch_shapes=[
            pltpu.VMEM((2, C), F32),
            pltpu.VMEM((2, 9, C, C), BF16),
            pltpu.VMEM((2, 3, C, C), BF16),
            vm(16, BF16, 9 * C),
            vm(14, BF16, 9 * C),
            vm(16, BF16),
            pltpu.SemaphoreType.DMA((5,)),
        ],
        compiler_params=pltpu.CompilerParams(vmem_limit_bytes=24 * 1024 * 1024),
        cost_estimate=pl.CostEstimate(
            flops=3_500_000_000, bytes_accessed=4_000_000, transcendentals=500_000
        ),
    )(video, gains, sw, tw)
    return pl.pallas_call(
        model_kernel,
        out_shape=(
            jax.ShapeDtypeStruct((128, 4 * C), BF16),
            OUT((FLAT, 128), BF16),
            OUT((FLAT, 128), BF16),
        ),
        in_specs=[pl.BlockSpec(memory_space=pltpu.SMEM)] + [whole] * 2 + [hbm] * 6 + [whole] * 3,
        out_specs=(whole, whole, whole),
        scratch_shapes=[
            vm(24, F32),
            vm(21, F32),
            vm(18, BF16, 9 * C),
            vm(16, BF16),
            vm(24, BF16),
            vm(21, BF16),
            vm(21, F32),
            vm(18, BF16),
            vm(11, BF16),
            vm(18, F32),
            vm(20, BF16),
            vm(18, BF16),
            vm(18, F32),
            vm(18, F32),
            pltpu.VMEM((C, 9 * C), BF16),
            pltpu.VMEM((2, C), F32),
            pltpu.VMEM((2, 9, C, C), BF16),
            pltpu.VMEM((2, 3, C, C), BF16),
            pltpu.VMEM((3, C, C), BF16),
            vm(16, BF16),
            vm(16, BF16),
            pltpu.VMEM((32, 4, 4 * C), BF16),
            pltpu.VMEM((8 * PIX, C), F32),
            pltpu.SemaphoreType.DMA((7,)),
        ],
        compiler_params=pltpu.CompilerParams(vmem_limit_bytes=30 * 1024 * 1024),
        cost_estimate=pl.CostEstimate(
            flops=9_000_000_000, bytes_accessed=6_000_000, transcendentals=1_000_000
        ),
    )(core, before, after, gains, sw, tw, rw, video, cot, *known)


def passed_along(value, axes, steps):
    count = lax.axis_size(axes)
    first, last = (max(0, -steps), min(count, count - steps))
    return lax.ppermute(value, axes, [(source, source + steps) for source in range(first, last)])


def position(x, y, core, z):
    return ((x // 2 * 4 + y) * 2 + core) * 16 + z % 8 * 2 + x % 2


def wide_groups():
    groups = []
    for fixed in range(4):
        for pair in range(4):
            ends = (2 * pair, 2 * pair + 1)
            groups.append([position(x, fixed, 0, z) for x in range(4) for z in ends])
            ends = (2 * pair + 1, 2 * pair + 2)
            groups.append([position(fixed, y, 1, z) for y in range(4) for z in ends])
    return groups


def cross_groups():
    groups = []
    for fixed in range(4):
        for z in range(8):
            groups.append([position(fixed, y, 0, z) for y in range(4)])
            groups.append([position(x, fixed, 1, z) for x in range(4)])
    return groups


def rest_groups():
    return [
        [position(x, y, core, z) for z in range(parity, 8, 2)]
        for x in range(4)
        for y in range(4)
        for core in range(2)
        for parity in range(2)
    ]


def exchange(value, groups):
    return lax.all_to_all(
        value, EVERY, split_axis=0, concat_axis=0, tiled=True, axis_index_groups=groups
    )


def to_all(value, groups):
    rows, cols = value.shape
    count = len(groups[0])
    copies = jnp.broadcast_to(value[None], (count, rows, cols)).reshape(count * rows, cols)
    return exchange(copies, groups)


def sum_parts(parts, groups):
    count = len(groups[0])
    parts = parts.reshape(count, parts.shape[0] // count, parts.shape[1])
    return jnp.sum(parts.astype(F32), axis=0).astype(BF16)


def place_kernel(core_ref, part_ref, gains_ref, *refs):
    sp_ref, tm_ref, dn_ref, gn_ref, buf, small, sems = refs[-7:]
    lanes = pl.ds(pl.multiple_of(core_ref[0] * 128, 128), 128)
    ours = part_ref[ROWS : ROWS + 16, :].astype(F32)[:2]
    theirs = gains_ref[ROWS : ROWS + 16, :].astype(F32)[:2]
    first_core = core_ref[0] == 0
    small[:, :128] = jnp.where(first_core, ours, theirs)
    small[:, 128:] = jnp.where(first_core, theirs, ours)
    copies = [pltpu.make_async_copy(small, gn_ref, sems.at[0])]
    copies[0].start()
    for target, first, spans in ((sp_ref, 0, (3, 5, 5, 5)), (tm_ref, 18, (6,)), (dn_ref, 24, (3,))):
        start = first
        for span in spans:
            for matrix in range(start, start + span):
                buf[matrix] = part_ref[pl.ds(matrix * C, C), :].astype(F32)
            copy = pltpu.make_async_copy(
                buf.at[pl.ds(start, span)],
                target.at[pl.ds(start - first, span), :, lanes],
                sems.at[len(copies)],
            )
            copy.start()
            copies.append(copy)
            start += span
    for copy in copies:
        copy.wait()


def place(which, part, gains, outputs=()):
    whole = pl.BlockSpec(memory_space=pltpu.VMEM)
    hbm = pl.BlockSpec(memory_space=HBM)
    return pl.pallas_call(
        place_kernel,
        out_shape=(
            jax.ShapeDtypeStruct((18, C, C), F32),
            jax.ShapeDtypeStruct((6, C, C), F32),
            jax.ShapeDtypeStruct((3, C, C), F32),
            jax.ShapeDtypeStruct((2, C), F32),
        ),
        in_specs=[pl.BlockSpec(memory_space=pltpu.SMEM), whole, whole] + [hbm] * len(outputs),
        out_specs=(hbm,) * 4,
        scratch_shapes=[
            pltpu.VMEM((MATS, C, 128), F32),
            pltpu.VMEM((2, C), F32),
            pltpu.SemaphoreType.DMA((7,)),
        ],
        input_output_aliases={3 + i: i for i in range(len(outputs))},
        compiler_params=pltpu.CompilerParams(vmem_limit_bytes=16 * 1024 * 1024),
        cost_estimate=pl.CostEstimate(flops=0, bytes_accessed=6_000_000, transcendentals=0),
    )(which, part, gains, *outputs)


def on_device(video, cotangent, gains, spatial_weights, time_weights, reduce_kernel_weights):
    tm = ("z", "xl")
    video, cot, gains, sw, tw, rw = (
        pltpu.with_memory_space_constraint(value, HBM)
        for value in (
            video.reshape(FR * PIX, C),
            cotangent.reshape(FR * 2, 4, 4 * C),
            gains,
            spatial_weights.reshape(2, 9, C, C),
            time_weights,
            reduce_kernel_weights,
        )
    )
    last, first = edges(video, cot)
    before = passed_along(last, tm, 1)
    after = passed_along(first, tm, -1)
    core = lax.axis_index("core").astype(jnp.int32).reshape(1)
    encoded, mine, theirs = run_model(
        core,
        video,
        before,
        after,
        cot,
        gains,
        sw,
        tw,
        rw,
    )
    swap = [(0, 1), (1, 0)]
    other = lax.ppermute(theirs, "core", swap)
    half = (mine.astype(F32) + other.astype(F32)).astype(BF16)
    wide, cross, rest = wide_groups(), cross_groups(), rest_groups()
    part = sum_parts(exchange(half, wide), wide)
    part = sum_parts(exchange(part, cross), cross)
    part = sum_parts(to_all(part, rest), rest)
    mine = to_all(to_all(part, cross), wide)
    other = lax.ppermute(mine, "core", swap)
    outputs = place(core, mine, mine)[:3]
    grad_sp, grad_tm, grad_dn, grad_gn = place(1 - core, other, mine, outputs)
    return (
        encoded.reshape(1, FR // 2, 4, 4, 4 * C),
        grad_sp.reshape(2, 3, 3, C, C),
        grad_tm.reshape(2, 3, C, C),
        grad_dn,
        grad_gn,
    )


def solution(mesh):
    fine = Mesh(mesh.devices.reshape(2, 4, 2, 8, 2), EVERY)
    split = P(("xh", "y", "core"), ("z", "xl"), None, None, None)
    return jax.shard_map(
        on_device,
        mesh=fine,
        in_specs=(split, split, P(), P(), P(), P()),
        out_specs=(split, P(), P(), P(), P()),
        check_vma=False,
    )
```

time: 140 us -> 120 us (0.86)
  blocking collectives: 84.3 us -> 70.4 us
  local copies, waits for them, and re-layouts: 7.98 us -> 3.2 us
  Pallas kernels: 29.1 us -> 25.8 us
  starting transfers between devices: 12.2 us -> 14.3 us
    all_to_all x4 -> x5, blocking collectives: 84.3 us -> 70.4 us  [exchange(): lax.all_to_all(value, EVERY, split_axis=0, concat_axis=0, tiled=True, axi...]
    pallas_call x1, Pallas kernels: 20.7 us -> 14.1 us  [run_model(): pl.pallas_call(model_kernel, out_shape=(jax.ShapeDtypeStruct((128, 4 * C)...]
    pallas_call x1 -> x2, Pallas kernels: 2.92 us -> 6.47 us  [the longest x1 5.46 us: run_model(): pl.pallas_call(front_kernel, out_shape=tuple((OUT((count * PIX, C), dtype...]
    slice x3 -> x0, local copies, waits for them, and re-layouts: 2.37 us -> none  [the longest x1 0.94 us: on_device(): before = passed_along(video[-6 * PIX:], tm, 1)]
    ppermute x1, starting transfers between devices: 1.25 us -> 3.29 us  [on_device(): other = lax.ppermute(theirs, 'core', swap)]
    unnamed x20 -> x4, local copies, waits for them, and re-layouts: 3.43 us -> 2.1 us
  transfers between devices with their start and end apart: 4 -> 4, of which waited for: 2 -> 2; matrix products, arithmetic and copies ran while one was open for 2% -> 1% of each run, Pallas kernels for 4% -> 6%
where the time goes in v4:
time: 120 us
  blocking collectives  70.4 us (59%)
  Pallas kernels  25.8 us (22%)
  starting transfers between devices  14.3 us (12%)
  waiting for transfers between devices  4.28 us (4%)
  local copies, waits for them, and re-layouts  3.2 us (3%)
    all_to_all x5, blocking collectives, exchange(): lax.all_to_all(value, EVERY, split_axis=0, concat_axis=0, tiled=True, axi...  70.4 us
    pallas_call x1, Pallas kernels, run_model(): pl.pallas_call(model_kernel, out_shape=(jax.ShapeDtypeStruct((128, 4 * C)...  14.1 us
    ppermute x2, starting transfers between devices, passed_along(): lax.ppermute(value, axes, [(source, source + steps) for source in range(f...  5.88 us
    pallas_call x1, Pallas kernels, run_model(): pl.pallas_call(front_kernel, out_shape=tuple((OUT((count * PIX, C), dtype...  5.46 us
    pallas_call x2, Pallas kernels, place(): pl.pallas_call(place_kernel, out_shape=(jax.ShapeDtypeStruct((18, C, C),...  5.23 us
    ppermute x1, starting transfers between devices, on_device(): other = lax.ppermute(mine, 'core', swap)  5.12 us
    ppermute x1, waiting for transfers between devices, on_device(): other = lax.ppermute(theirs, 'core', swap)  3.41 us
    ppermute x1, starting transfers between devices, on_device(): other = lax.ppermute(theirs, 'core', swap)  3.29 us
  transfers between devices with their start and end apart: 4, of which 2 were waited for; matrix products, arithmetic and copies ran while one was open for 1% of the time, Pallas kernels for 6%

profile of v4, /device:TPU:1, one launch (start us, length us, event | category | flops | bytes accessed | tf_op | source)
XLA Modules:
  0.0 119.7 jit_solution(1075361490229444020)
XLA Ops:
  0.6 1.0 shard_map.101
  1.6 1.3 %collective-permute-start.1 = (bf16[320,256]{1,0:T(8,128)(2,1)S(1)}, bf16[320,256]{1,0:T(8,128)(2,1)S(1)}, u32[]{:S(2)}, u32[]{:S(2)}) collective-permute-start(bf16[320,256]{1,0:T(8,128)(2,1)S(1)} %get-tuple-element.21), channel_id=1, source_target_pairs={{1,0},{2,1},{3,2},{4,3},{5,4},{6,5},{7,6},{8,7},{9,8},{10,9},{11,1... | collective-permute-start | bytes 491528 | tf_op jit(solution)/shard_map/ppermute | solution.py:471
  2.9 4.6 %collective-permute-start = (bf16[384,256]{1,0:T(8,128)(2,1)S(1)}, bf16[384,256]{1,0:T(8,128)(2,1)S(1)}, u32[]{:S(2)}, u32[]{:S(2)}) collective-permute-start(bf16[384,256]{1,0:T(8,128)(2,1)S(1)} %get-tuple-element.20), channel_id=1, source_target_pairs={{0,1},{1,2},{2,3},{3,4},{4,5},{5,6},{6,7},{7,8},{8,9},{9,10},{10,1... | collective-permute-start | bytes 589832 | tf_op jit(solution)/shard_map/ppermute | solution.py:471
  7.5 5.5 %shard_map.102 = (bf16[2816,256]{1,0:T(8,128)(2,1)S(1)}, f32[1024,256]{1,0:T(8,128)S(1)}, f32[896,256]{1,0:T(8,128)S(1)}) custom-call(bf16[1024,256]{1,0:T(8,128)(2,1)} %bitcast.20, f32[2,256]{1,0:T(2,128)} %gains_hbm.3, bf16[2,9,256,256]{3,2,1,0:T(8,128)(2,1)} %bitcast.24, bf16[2,3,256,256]{3,2,1,0:T(8,128)(2,1)} %tw_hbm.3), custom_call_target="tpu_custom_call" | custom-call | flops 3500000000 | bytes 4000000 | tf_op jit(solution)/shard_map/pallas_call | solution.py:407
  13.0 0.0 copy-start
  13.0 0.9 copy-done
  13.9 0.0 collective-permute-done.1.after_ref
  13.9 0.0 collective-permute-done.before_ref
  13.9 0.0 copy-start.1
  13.9 1.2 copy-done.1
  15.1 14.1 %shard_map.103 = (bf16[128,1024]{1,0:T(8,128)(2,1)S(1)}, bf16[7168,128]{1,0:T(8,128)(2,1)S(1)}, bf16[7168,128]{1,0:T(8,128)(2,1)S(1)}) custom-call(s32[1]{0:T(128)} %bitcast.core_ref, bf16[384,256]{1,0:T(8,128)(2,1)S(1)} %collective-permute-done.before_ref, bf16[320,256]{1,0:T(8,128)(2,1)S(1)} %collective-permute-done.1.after_ref, f32[2,256]{1,0:T(2,128)} %gains_hbm.3, ...), custom_call_target="tpu_custom_call" | custom-call | flops 8999999488 | bytes 6000000 | tf_op jit(solution)/shard_map/pallas_call | solution.py:426
  29.3 3.3 %collective-permute-start.2 = (bf16[7168,128]{1,0:T(8,128)(2,1)S(1)}, bf16[7168,128]{1,0:T(8,128)(2,1)S(1)}, u32[]{:S(2)}, u32[]{:S(2)}) collective-permute-start(bf16[7168,128]{1,0:T(8,128)(2,1)S(1)} %get-tuple-element.27), channel_id=1, source_target_pairs={{0,16},{16,0},{1,17},{17,1},{2,18},{18,2},{3,19},{19,3},{4,20},{20... | collective-permute-start | bytes 5505032 | tf_op jit(solution)/shard_map/ppermute | solution.py:607
  32.5 3.4 %collective-permute-done.2 = bf16[7168,128]{1,0:T(8,128)(2,1)S(1)} collective-permute-done((bf16[7168,128]{1,0:T(8,128)(2,1)S(1)}, bf16[7168,128]{1,0:T(8,128)(2,1)S(1)}, u32[]{:S(2)}, u32[]{:S(2)}) %collective-permute-start.2) | collective-permute-done | bytes 1835040 | tf_op jit(solution)/shard_map/ppermute | solution.py:607
  36.0 0.5 add_convert_fusion
  36.4 22.3 %all_to_all.38 = bf16[8,896,128]{2,1,0:T(8,128)(2,1)S(1)} all-to-all(bf16[8,896,128]{2,1,0:T(8,128)(2,1)S(1)} %bitcast.14), channel_id=1, replica_groups={{0,2,1,3,128,130,129,131},{18,20,50,52,82,84,114,116},{4,6,5,7,132,134,..., dimensions={0} | all-to-all | bytes 3670016 | tf_op jit(solution)/shard_map/all_to_all | solution.py:509
  58.7 0.3 reduce_sum.36
  59.0 8.9 %all_to_all.39 = bf16[4,224,128]{2,1,0:T(8,128)(2,1)S(1)} all-to-all(bf16[4,224,128]{2,1,0:T(8,128)(2,1)S(1)} %bitcast.17), channel_id=1, replica_groups={{0,32,64,96},{16,17,144,145},{2,34,66,98},{18,19,146,147},{4,36,68,100}..., dimensions={0} | all-to-all | bytes 458752 | tf_op jit(solution)/shard_map/all_to_all | solution.py:509
  68.0 13.2 %all_to_all.40 = bf16[4,224,128]{2,1,0:T(8,128)(2,1)S(1)} all-to-all(bf16[4,224,128]{2,1,0:T(8,128)(2,1)S(1)} %broadcast_in_dim.8), channel_id=1, replica_groups={{0,4,8,12},{2,6,10,14},{16,20,24,28},{18,22,26,30},{32,36,40,44},{34,38..., dimensions={0} | all-to-all | bytes 458752 | tf_op jit(solution)/shard_map/all_to_all | solution.py:509
  81.3 7.7 %all_to_all.41 = bf16[4,224,128]{2,1,0:T(8,128)(2,1)S(1)} all-to-all(bf16[4,224,128]{2,1,0:T(8,128)(2,1)S(1)} %broadcast_in_dim.9), channel_id=1, replica_groups={{0,32,64,96},{16,17,144,145},{2,34,66,98},{18,19,146,147},{4,36,68,100}..., dimensions={0} | all-to-all | bytes 458752 | tf_op jit(solution)/shard_map/all_to_all | solution.py:509
  89.0 0.2 broadcast_in_dim.11
  89.2 18.3 %all_to_all.42 = bf16[8,896,128]{2,1,0:T(8,128)(2,1)S(1)} all-to-all(bf16[8,896,128]{2,1,0:T(8,128)(2,1)S(1)} %broadcast_in_dim.11), channel_id=1, replica_groups={{0,2,1,3,128,130,129,131},{18,20,50,52,82,84,114,116},{4,6,5,7,132,134,..., dimensions={0} | all-to-all | bytes 3670016 | tf_op jit(solution)/shard_map/all_to_all | solution.py:509
  107.6 5.1 %collective-permute-start.3 = (bf16[7168,128]{1,0:T(8,128)(2,1)S(1)}, bf16[7168,128]{1,0:T(8,128)(2,1)}, u32[]{:S(2)}, u32[]{:S(2)}) collective-permute-start(bf16[7168,128]{1,0:T(8,128)(2,1)S(1)} %bitcast.10), channel_id=1, source_target_pairs={{0,16},{16,0},{1,17},{17,1},{2,18},{18,2},{3,19},{19,3},{4,20},{20... | collective-permute-start | bytes 5505032 | tf_op jit(solution)/shard_map/ppermute | solution.py:614
  112.7 0.8 reshape.61
  113.5 1.9 %shard_map.104 = (f32[18,256,256]{2,1,0:T(8,128)}, f32[6,256,256]{2,1,0:T(8,128)}, f32[3,256,256]{2,1,0:T(8,128)}, f32[2,256]{1,0:T(2,128)}) custom-call(s32[1]{0:T(128)} %bitcast.core_ref, bf16[7168,128]{1,0:T(8,128)(2,1)S(1)} %bitcast.11, bf16[7168,128]{1,0:T(8,128)(2,1)S(1)} %bitcast.12), custom_call_target="tpu_custom_call" | custom-call | bytes 6000000 | tf_op jit(solution)/shard_map/pallas_call | solution.py:557
  115.4 0.9 collective-permute-done.3.part_ref
  116.2 3.4 %shard_map.105 = (f32[18,256,256]{2,1,0:T(8,128)}, f32[6,256,256]{2,1,0:T(8,128)}, f32[3,256,256]{2,1,0:T(8,128)}, f32[2,256]{1,0:T(2,128)}) custom-call(s32[1]{0:T(128)S(6)} %sub.3.core_ref, bf16[7168,128]{1,0:T(8,128)(2,1)} %collective-permute-done.3.part_ref, ...), custom_call_target="tpu_custom_call", output_to_operand_aliasing={{0}: (3, {}), {1}: (4, {}), {2}: (5, {})} | custom-call | bytes 6000000 | tf_op jit(solution)/shard_map/pallas_call | solution.py:557
  (4 shorter events, 0.1 us)
Async XLA Ops:
  1.6 12.3 %collective-permute-start.1 = (bf16[320,256]{1,0:T(8,128)(2,1)S(1)}, bf16[320,256]{1,0:T(8,128)(2,1)S(1)}, u32[]{:S(2)}, u32[]{:S(2)}) collective-permute-start(bf16[320,256]{1,0:T(8,128)(2,1)S(1)} %get-tuple-element.21), channel_id=1, source_target_pairs={{1,0},{2,1},{3,2},{4,3},{5,4},{6,5},{7,6},{8,7},{9,8},{10,9},{11,1... | collective-permute-start | bytes 491528 | tf_op jit(solution)/shard_map/ppermute | solution.py:471
  2.9 11.0 %collective-permute-start = (bf16[384,256]{1,0:T(8,128)(2,1)S(1)}, bf16[384,256]{1,0:T(8,128)(2,1)S(1)}, u32[]{:S(2)}, u32[]{:S(2)}) collective-permute-start(bf16[384,256]{1,0:T(8,128)(2,1)S(1)} %get-tuple-element.20), channel_id=1, source_target_pairs={{0,1},{1,2},{2,3},{3,4},{4,5},{5,6},{6,7},{7,8},{8,9},{9,10},{10,1... | collective-permute-start | bytes 589832 | tf_op jit(solution)/shard_map/ppermute | solution.py:471
  13.0 0.9 copy-start
  13.9 1.2 copy-start.1
  29.3 6.7 %collective-permute-start.2 = (bf16[7168,128]{1,0:T(8,128)(2,1)S(1)}, bf16[7168,128]{1,0:T(8,128)(2,1)S(1)}, u32[]{:S(2)}, u32[]{:S(2)}) collective-permute-start(bf16[7168,128]{1,0:T(8,128)(2,1)S(1)} %get-tuple-element.27), channel_id=1, source_target_pairs={{0,16},{16,0},{1,17},{17,1},{2,18},{18,2},{3,19},{19,3},{4,20},{20... | collective-permute-start | bytes 5505032 | tf_op jit(solution)/shard_map/ppermute | solution.py:607
  107.6 8.7 %collective-permute-start.3 = (bf16[7168,128]{1,0:T(8,128)(2,1)S(1)}, bf16[7168,128]{1,0:T(8,128)(2,1)}, u32[]{:S(2)}, u32[]{:S(2)}) collective-permute-start(bf16[7168,128]{1,0:T(8,128)(2,1)S(1)} %bitcast.10), channel_id=1, source_target_pairs={{0,16},{16,0},{1,17},{17,1},{2,18},{18,2},{3,19},{19,3},{4,20},{20... | collective-permute-start | bytes 5505032 | tf_op jit(solution)/shard_map/ppermute | solution.py:614

commit v5 on v4

--- a/solution.py
+++ b/solution.py
@@ -167,10 +167,10 @@
     tw_hbm,
     pack_ref,
     slope1_ref,
-    s2_ref,
     gains,
     sw_ref,
     tw_ref,
+    s2_ref,
     im1,
     im2,
     video,
@@ -211,7 +211,6 @@
     cot_hbm,
     pack_ref,
     slope1,
-    s2_own,
     enc_ref,
     mine_ref,
     theirs_ref,
@@ -256,7 +255,6 @@
     s1[frames(22, 2), :] = after_ref[: 2 * PIX].astype(F32)
     a1_own, a2_own, slope2_own = unpacked(pack_ref)
     a1[frames(6, 16), :] = a1_own[...]
-    s2[frames(5, 14), :] = s2_own[...]
     a2[frames(5, 14), :] = a2_own[...]
     slope2[frames(5, 14), :] = slope2_own[...].astype(F32)
     n_refs = (n1_ref, n2_ref)
@@ -278,6 +276,8 @@
         copy.wait()
     activate(im, sw_ref[0], [(0, 384, 0, None), (384, 128, 1408, None)], a1, None)
     norm_only(s1_own, 0, FR, gains_ref[0:1, :], n1_ref, 0)
+    middle = dot(with_edge(a1, 8, 14), tw_ref[0].reshape(3 * C, C))
+    s2[frames(5, 14), :] = s1_own[frames(2, 14), :].astype(F32) + middle
     norm_only(s2, 5, 14, gains_ref[1:2, :], n2_ref, 2)
     side_by_side(cot_raw, 32, cot_flat)
     ends = jnp.concatenate([with_edge(a1, 3, 5), with_edge(a1, 22, 2)], axis=0)
@@ -403,16 +403,17 @@
 
     whole = pl.BlockSpec(memory_space=pltpu.VMEM)
     hbm = pl.BlockSpec(memory_space=HBM)
-    own = [(44, BF16), (16, F32), (14, F32)]
+    own = [(44, BF16), (16, F32)]
     known = pl.pallas_call(
         front_kernel,
         out_shape=tuple(OUT((count * PIX, C), dtype) for count, dtype in own),
         in_specs=[hbm] * 4,
-        out_specs=(whole,) * 3,
+        out_specs=(whole,) * 2,
         scratch_shapes=[
             pltpu.VMEM((2, C), F32),
             pltpu.VMEM((2, 9, C, C), BF16),
             pltpu.VMEM((2, 3, C, C), BF16),
+            vm(14, F32),
             vm(16, BF16, 9 * C),
             vm(14, BF16, 9 * C),
             vm(16, BF16),
@@ -430,7 +431,7 @@
             OUT((FLAT, 128), BF16),
             OUT((FLAT, 128), BF16),
         ),
-        in_specs=[pl.BlockSpec(memory_space=pltpu.SMEM)] + [whole] * 2 + [hbm] * 6 + [whole] * 3,
+        in_specs=[pl.BlockSpec(memory_space=pltpu.SMEM)] + [whole] * 2 + [hbm] * 6 + [whole] * 2,
         out_specs=(whole, whole, whole),
         scratch_shapes=[
             vm(24, F32),

time: 120 us -> 119 us (level)
  local copies, waits for them, and re-layouts: 3.2 us -> 1.1 us
    unnamed x4 -> x0, local copies, waits for them, and re-layouts: 2.1 us -> none
  transfers between devices with their start and end apart: 4 -> 4, of which waited for: 2 -> 3; matrix products, arithmetic and copies ran while one was open for 1% -> 1% of each run, Pallas kernels for 6% -> 6%
where the time goes in v5:
time: 119 us
  blocking collectives  71.3 us (60%)
  Pallas kernels  25.9 us (22%)
  starting transfers between devices  13.7 us (12%)
  waiting for transfers between devices  4.98 us (4%)
    all_to_all x5, blocking collectives, exchange(): lax.all_to_all(value, EVERY, split_axis=0, concat_axis=0, tiled=True, axi...  71.3 us
    pallas_call x1, Pallas kernels, run_model(): pl.pallas_call(model_kernel, out_shape=(jax.ShapeDtypeStruct((128, 4 * C)...  14.2 us
    ppermute x2, starting transfers between devices, passed_along(): lax.ppermute(value, axes, [(source, source + steps) for source in range(f...  5.88 us
    pallas_call x1, Pallas kernels, run_model(): pl.pallas_call(front_kernel, out_shape=tuple((OUT((count * PIX, C), dtype...  5.47 us
    pallas_call x2, Pallas kernels, place(): pl.pallas_call(place_kernel, out_shape=(jax.ShapeDtypeStruct((18, C, C),...  5.23 us
    ppermute x1, starting transfers between devices, on_device(): other = lax.ppermute(mine, 'core', swap)  5.16 us
    ppermute x1, waiting for transfers between devices, on_device(): other = lax.ppermute(theirs, 'core', swap)  3.41 us
    ppermute x1, starting transfers between devices, on_device(): other = lax.ppermute(theirs, 'core', swap)  2.62 us
  transfers between devices with their start and end apart: 4, of which 3 were waited for; matrix products, arithmetic and copies ran while one was open for 1% of the time, Pallas kernels for 6%

profile of v5, /device:TPU:1, one launch (start us, length us, event | category | flops | bytes accessed | tf_op | source)
XLA Modules:
  0.0 118.7 jit_solution(5774815238580510394)
XLA Ops:
  0.6 1.0 shard_map.101
  1.6 1.3 %collective-permute-start.1 = (bf16[320,256]{1,0:T(8,128)(2,1)S(1)}, bf16[320,256]{1,0:T(8,128)(2,1)S(1)}, u32[]{:S(2)}, u32[]{:S(2)}) collective-permute-start(bf16[320,256]{1,0:T(8,128)(2,1)S(1)} %get-tuple-element.20), channel_id=1, source_target_pairs={{1,0},{2,1},{3,2},{4,3},{5,4},{6,5},{7,6},{8,7},{9,8},{10,9},{11,1... | collective-permute-start | bytes 491528 | tf_op jit(solution)/shard_map/ppermute | solution.py:472
  2.9 4.6 %collective-permute-start = (bf16[384,256]{1,0:T(8,128)(2,1)S(1)}, bf16[384,256]{1,0:T(8,128)(2,1)S(1)}, u32[]{:S(2)}, u32[]{:S(2)}) collective-permute-start(bf16[384,256]{1,0:T(8,128)(2,1)S(1)} %get-tuple-element.19), channel_id=1, source_target_pairs={{0,1},{1,2},{2,3},{3,4},{4,5},{5,6},{6,7},{7,8},{8,9},{9,10},{10,1... | collective-permute-start | bytes 589832 | tf_op jit(solution)/shard_map/ppermute | solution.py:472
  7.5 5.5 %shard_map.102 = (bf16[2816,256]{1,0:T(8,128)(2,1)S(1)}, f32[1024,256]{1,0:T(8,128)S(1)}) custom-call(bf16[1024,256]{1,0:T(8,128)(2,1)} %bitcast.20, f32[2,256]{1,0:T(2,128)} %gains_hbm.3, bf16[2,9,256,256]{3,2,1,0:T(8,128)(2,1)} %bitcast.24, bf16[2,3,256,256]{3,2,1,0:T(8,128)(2,1)} %tw_hbm.3), custom_call_target="tpu_custom_call" | custom-call | flops 3500000000 | bytes 4000000 | tf_op jit(solution)/shard_map/pallas_call | solution.py:407
  13.0 0.0 collective-permute-done.1.after_ref
  13.0 0.7 collective-permute-done.before_ref
  13.7 14.2 %shard_map.103 = (bf16[128,1024]{1,0:T(8,128)(2,1)S(1)}, bf16[7168,128]{1,0:T(8,128)(2,1)S(1)}, bf16[7168,128]{1,0:T(8,128)(2,1)S(1)}) custom-call(s32[1]{0:T(128)} %bitcast.core_ref, bf16[384,256]{1,0:T(8,128)(2,1)S(1)} %collective-permute-done.before_ref, bf16[320,256]{1,0:T(8,128)(2,1)S(1)} %collective-permute-done.1.after_ref, f32[2,256]{1,0:T(2,128)} %gains_hbm.3, ...), custom_call_target="tpu_custom_call" | custom-call | flops 8999999488 | bytes 6000000 | tf_op jit(solution)/shard_map/pallas_call | solution.py:427
  27.9 2.6 %collective-permute-start.2 = (bf16[7168,128]{1,0:T(8,128)(2,1)S(1)}, bf16[7168,128]{1,0:T(8,128)(2,1)S(1)}, u32[]{:S(2)}, u32[]{:S(2)}) collective-permute-start(bf16[7168,128]{1,0:T(8,128)(2,1)S(1)} %get-tuple-element.25), channel_id=1, source_target_pairs={{0,16},{16,0},{1,17},{17,1},{2,18},{18,2},{3,19},{19,3},{4,20},{20... | collective-permute-start | bytes 5505032 | tf_op jit(solution)/shard_map/ppermute | solution.py:608
  30.5 3.4 %collective-permute-done.2 = bf16[7168,128]{1,0:T(8,128)(2,1)S(1)} collective-permute-done((bf16[7168,128]{1,0:T(8,128)(2,1)S(1)}, bf16[7168,128]{1,0:T(8,128)(2,1)S(1)}, u32[]{:S(2)}, u32[]{:S(2)}) %collective-permute-start.2) | collective-permute-done | bytes 1835040 | tf_op jit(solution)/shard_map/ppermute | solution.py:608
  33.9 0.5 add_convert_fusion
  34.4 23.1 %all_to_all.38 = bf16[8,896,128]{2,1,0:T(8,128)(2,1)S(1)} all-to-all(bf16[8,896,128]{2,1,0:T(8,128)(2,1)S(1)} %bitcast.14), channel_id=1, replica_groups={{0,2,1,3,128,130,129,131},{18,20,50,52,82,84,114,116},{4,6,5,7,132,134,..., dimensions={0} | all-to-all | bytes 3670016 | tf_op jit(solution)/shard_map/all_to_all | solution.py:510
  57.5 0.3 reduce_sum.36
  57.9 8.9 %all_to_all.39 = bf16[4,224,128]{2,1,0:T(8,128)(2,1)S(1)} all-to-all(bf16[4,224,128]{2,1,0:T(8,128)(2,1)S(1)} %bitcast.17), channel_id=1, replica_groups={{0,32,64,96},{16,17,144,145},{2,34,66,98},{18,19,146,147},{4,36,68,100}..., dimensions={0} | all-to-all | bytes 458752 | tf_op jit(solution)/shard_map/all_to_all | solution.py:510
  66.8 13.2 %all_to_all.40 = bf16[4,224,128]{2,1,0:T(8,128)(2,1)S(1)} all-to-all(bf16[4,224,128]{2,1,0:T(8,128)(2,1)S(1)} %broadcast_in_dim.8), channel_id=1, replica_groups={{0,4,8,12},{2,6,10,14},{16,20,24,28},{18,22,26,30},{32,36,40,44},{34,38..., dimensions={0} | all-to-all | bytes 458752 | tf_op jit(solution)/shard_map/all_to_all | solution.py:510
  80.1 7.7 %all_to_all.41 = bf16[4,224,128]{2,1,0:T(8,128)(2,1)S(1)} all-to-all(bf16[4,224,128]{2,1,0:T(8,128)(2,1)S(1)} %broadcast_in_dim.9), channel_id=1, replica_groups={{0,32,64,96},{16,17,144,145},{2,34,66,98},{18,19,146,147},{4,36,68,100}..., dimensions={0} | all-to-all | bytes 458752 | tf_op jit(solution)/shard_map/all_to_all | solution.py:510
  87.9 0.2 broadcast_in_dim.11
  88.1 18.3 %all_to_all.42 = bf16[8,896,128]{2,1,0:T(8,128)(2,1)S(1)} all-to-all(bf16[8,896,128]{2,1,0:T(8,128)(2,1)S(1)} %broadcast_in_dim.11), channel_id=1, replica_groups={{0,2,1,3,128,130,129,131},{18,20,50,52,82,84,114,116},{4,6,5,7,132,134,..., dimensions={0} | all-to-all | bytes 3670016 | tf_op jit(solution)/shard_map/all_to_all | solution.py:510
  106.4 5.2 %collective-permute-start.3 = (bf16[7168,128]{1,0:T(8,128)(2,1)S(1)}, bf16[7168,128]{1,0:T(8,128)(2,1)}, u32[]{:S(2)}, u32[]{:S(2)}) collective-permute-start(bf16[7168,128]{1,0:T(8,128)(2,1)S(1)} %bitcast.10), channel_id=1, source_target_pairs={{0,16},{16,0},{1,17},{17,1},{2,18},{18,2},{3,19},{19,3},{4,20},{20... | collective-permute-start | bytes 5505032 | tf_op jit(solution)/shard_map/ppermute | solution.py:615
  111.6 0.8 reshape.61
  112.4 1.9 %shard_map.104 = (f32[18,256,256]{2,1,0:T(8,128)}, f32[6,256,256]{2,1,0:T(8,128)}, f32[3,256,256]{2,1,0:T(8,128)}, f32[2,256]{1,0:T(2,128)}) custom-call(s32[1]{0:T(128)} %bitcast.core_ref, bf16[7168,128]{1,0:T(8,128)(2,1)S(1)} %bitcast.11, bf16[7168,128]{1,0:T(8,128)(2,1)S(1)} %bitcast.12), custom_call_target="tpu_custom_call" | custom-call | bytes 6000000 | tf_op jit(solution)/shard_map/pallas_call | solution.py:558
  114.3 0.9 collective-permute-done.3.part_ref
  115.1 3.4 %shard_map.105 = (f32[18,256,256]{2,1,0:T(8,128)}, f32[6,256,256]{2,1,0:T(8,128)}, f32[3,256,256]{2,1,0:T(8,128)}, f32[2,256]{1,0:T(2,128)}) custom-call(s32[1]{0:T(128)S(6)} %sub.3.core_ref, bf16[7168,128]{1,0:T(8,128)(2,1)} %collective-permute-done.3.part_ref, ...), custom_call_target="tpu_custom_call", output_to_operand_aliasing={{0}: (3, {}), {1}: (4, {}), {2}: (5, {})} | custom-call | bytes 6000000 | tf_op jit(solution)/shard_map/pallas_call | solution.py:558
  (4 shorter events, 0.1 us)
Async XLA Ops:
  1.6 11.4 %collective-permute-start.1 = (bf16[320,256]{1,0:T(8,128)(2,1)S(1)}, bf16[320,256]{1,0:T(8,128)(2,1)S(1)}, u32[]{:S(2)}, u32[]{:S(2)}) collective-permute-start(bf16[320,256]{1,0:T(8,128)(2,1)S(1)} %get-tuple-element.20), channel_id=1, source_target_pairs={{1,0},{2,1},{3,2},{4,3},{5,4},{6,5},{7,6},{8,7},{9,8},{10,9},{11,1... | collective-permute-start | bytes 491528 | tf_op jit(solution)/shard_map/ppermute | solution.py:472
  2.9 10.8 %collective-permute-start = (bf16[384,256]{1,0:T(8,128)(2,1)S(1)}, bf16[384,256]{1,0:T(8,128)(2,1)S(1)}, u32[]{:S(2)}, u32[]{:S(2)}) collective-permute-start(bf16[384,256]{1,0:T(8,128)(2,1)S(1)} %get-tuple-element.19), channel_id=1, source_target_pairs={{0,1},{1,2},{2,3},{3,4},{4,5},{5,6},{6,7},{7,8},{8,9},{9,10},{10,1... | collective-permute-start | bytes 589832 | tf_op jit(solution)/shard_map/ppermute | solution.py:472
  27.9 6.0 %collective-permute-start.2 = (bf16[7168,128]{1,0:T(8,128)(2,1)S(1)}, bf16[7168,128]{1,0:T(8,128)(2,1)S(1)}, u32[]{:S(2)}, u32[]{:S(2)}) collective-permute-start(bf16[7168,128]{1,0:T(8,128)(2,1)S(1)} %get-tuple-element.25), channel_id=1, source_target_pairs={{0,16},{16,0},{1,17},{17,1},{2,18},{18,2},{3,19},{19,3},{4,20},{20... | collective-permute-start | bytes 5505032 | tf_op jit(solution)/shard_map/ppermute | solution.py:608
  106.4 8.7 %collective-permute-start.3 = (bf16[7168,128]{1,0:T(8,128)(2,1)S(1)}, bf16[7168,128]{1,0:T(8,128)(2,1)}, u32[]{:S(2)}, u32[]{:S(2)}) collective-permute-start(bf16[7168,128]{1,0:T(8,128)(2,1)S(1)} %bitcast.10), channel_id=1, source_target_pairs={{0,16},{16,0},{1,17},{17,1},{2,18},{18,2},{3,19},{19,3},{4,20},{20... | collective-permute-start | bytes 5505032 | tf_op jit(solution)/shard_map/ppermute | solution.py:615
